TPU v7x, 256 devices: a whole 4x4x8 slice. The times are simulated.
256 devices in a mesh: row: 8 (over y_hi, x), col: 32 (over z, y_lo, core).
Axes of the slice: x: 4, y: 4 (y_hi: 2, y_lo: 2; y = y_hi * 2 + y_lo), z: 8, core: 2. Of those that a mesh axis runs over, the one named last changes fastest.
Arguments:
- query_pair: bfloat16 [8, 4096, 128], P('row', 'col'), may hold values from -40 to 40
- key_pair: bfloat16 [8, 4096, 128], P('row', 'col'), may hold values from -4 to 4
- value_pair: bfloat16 [8, 4096, 128], P('row', 'col'), may hold values from -6 to 6
- pair_bias: bfloat16 [4, 4096, 4096], P(None, 'col', 'row'), may hold values from -9 to 9
- residue_mask: int32 [4096], P('row'), may hold values from 0 to 1, as said below
- grad_output: bfloat16 [8, 4096, 128], P('row', 'col'), may hold values from -6 to 6
Outputs:
- grad_query: float32 [8, 4096, 128], P('row', 'col')
- grad_key: float32 [8, 4096, 128], P('row', 'col')
- grad_value: float32 [8, 4096, 128], P('row', 'col')
- grad_bias: float32 [4, 4096, 4096], P(None, 'col', 'row')
Inputs may be any that keep to these rules, and one draw needn't show every extreme that they name: `residue_mask`: residue 0 is present.
All inputs are finite; a program needn't handle non-finite values.
Results may differ from a plain program's by a relative error of at most 0.01.
Values may be sent and summed in bfloat16 or wider, within the bound.
A program may use at most 64 MiB of HBM per device.

v0:
```python
import math

import jax
import jax.numpy as jnp
from jax import lax
from jax.sharding import PartitionSpec as P

HEADS = 4
HEAD_DIM = 32


def shifted(value, axis, steps):
    count = lax.axis_size(axis)
    pairs = [(source, (source + steps) % count) for source in range(count)]
    return lax.ppermute(value, axis, pairs)


def on_device(query_pair, key_pair, value_pair, pair_bias, residue_mask, grad_output):
    col_local = query_pair.shape[1]
    channels = query_pair.shape[2]
    col_count = lax.axis_size("col")
    score_scale = 1.0 / math.sqrt(HEAD_DIM)
    stacked = jnp.stack([key_pair, value_pair])
    floor_low = jnp.asarray(-1000000000.0, jnp.bfloat16)
    bias_full, mask_full = (
        lax.all_gather(pair_bias, "row", axis=2, tiled=True),
        lax.all_gather(residue_mask.astype(jnp.bfloat16), "row", axis=0, tiled=True),
    )
    masked_bias = jnp.where(mask_full[None, None, :] > 0, bias_full, floor_low)
    row_count = query_pair.shape[0]
    query_heads = query_pair.reshape(row_count, col_local, HEADS, HEAD_DIM)
    grad_heads = grad_output.reshape(row_count, col_local, HEADS, HEAD_DIM)

    def scores_of(tile_kv, offset):
        length = tile_kv.shape[2]
        key_heads = tile_kv[0].reshape(row_count, length, HEADS, HEAD_DIM)
        bias_tile = lax.dynamic_slice_in_dim(masked_bias, offset, length, 2).astype(jnp.float32)
        products = jnp.einsum(
            "rjhd,rkhd->hrjk", query_heads, key_heads, preferred_element_type=jnp.float32
        )
        return products * score_scale + bias_tile[:, None]

    tile_kv = lax.all_gather(stacked, "col", axis=2, tiled=True)
    running_max = jnp.full((HEADS, row_count, col_local), -1e30, jnp.float32)
    length = tile_kv.shape[2]
    scores = scores_of(tile_kv, jnp.int32(0))
    new_max = jnp.maximum(running_max, jnp.max(scores, axis=-1))
    expo = jnp.exp(scores - new_max[..., None])
    value_heads = tile_kv[1].reshape(row_count, length, HEADS, HEAD_DIM).astype(jnp.float32)
    added = jnp.einsum("hrjk,rkhd->hrjd", expo, value_heads, precision=lax.Precision.HIGHEST)
    running_sum = jnp.sum(expo, axis=-1)
    log_norm = new_max + jnp.log(running_sum)
    attended = added / running_sum[..., None]
    row_delta = jnp.sum(
        jnp.transpose(grad_heads, (2, 0, 1, 3)).astype(jnp.float32) * attended, axis=-1
    )

    def backward_block(tile_kv, offset):
        length = tile_kv.shape[2]
        key_heads = tile_kv[0].reshape(row_count, length, HEADS, HEAD_DIM)
        value_heads = tile_kv[1].reshape(row_count, length, HEADS, HEAD_DIM)
        weights = jnp.exp(scores_of(tile_kv, offset) - log_norm[..., None])
        weight_grad = jnp.einsum(
            "rjhd,rkhd->hrjk", grad_heads, value_heads, preferred_element_type=jnp.float32
        )
        score_grad = weights * (weight_grad - row_delta[..., None])
        weights_low = weights.astype(jnp.bfloat16)
        score_low = score_grad.astype(jnp.bfloat16)
        query_part = jnp.einsum(
            "hrjk,rkhd->rjhd", score_low, key_heads, preferred_element_type=jnp.float32
        )
        key_part = jnp.einsum(
            "hrjk,rjhd->rkhd", score_low, query_heads, preferred_element_type=jnp.float32
        )
        value_part = jnp.einsum(
            "hrjk,rjhd->rkhd", weights_low, grad_heads, preferred_element_type=jnp.float32
        )
        pair_part = jnp.stack(
            [
                key_part.reshape(row_count, length, channels),
                value_part.reshape(row_count, length, channels),
            ]
        )
        return (query_part, pair_part, jnp.sum(score_grad, axis=1))

    query_zero = jnp.zeros((row_count, col_local, HEADS, HEAD_DIM), jnp.float32)
    key_total = col_local * col_count

    def circulate_backward(rotation, carried):
        tile_kv, pair_acc, query_acc, bias_acc = carried
        anchor = (lax.axis_index("col") - rotation) % col_count
        offset = anchor * col_local
        query_part, pair_part, bias_part = backward_block(tile_kv, offset)
        bias_acc = lax.dynamic_update_slice_in_dim(bias_acc, bias_part, offset, 2)
        tile_kv = shifted(tile_kv, "col", 1)
        pair_acc = shifted(pair_acc + pair_part, "col", 1)
        return (tile_kv, pair_acc, query_acc + query_part, bias_acc)

    pair_zero = jnp.zeros((2, row_count, col_local, channels), jnp.float32)
    bias_zero = jnp.zeros((HEADS, col_local, key_total), jnp.float32)
    carried = lax.fori_loop(
        0, col_count, circulate_backward, (stacked, pair_zero, query_zero, bias_zero)
    )
    pair_grads = carried[1]
    query_acc = carried[2]
    bias_acc = carried[3]
    grad_bias = lax.psum_scatter(bias_acc, "row", scatter_dimension=2, tiled=True)
    query_sum = query_acc.reshape(row_count, col_local, channels)
    grad_query = query_sum * score_scale
    return (grad_query, pair_grads[0] * score_scale, pair_grads[1], grad_bias)


def solution(mesh):
    in_specs = (
        P("row", "col", None),
        P("row", "col", None),
        P("row", "col", None),
        P(None, "col", "row"),
        P("row"),
        P("row", "col", None),
    )
    out_specs = (
        P("row", "col", None),
        P("row", "col", None),
        P("row", "col", None),
        P(None, "col", "row"),
    )
    return jax.shard_map(
        on_device, mesh=mesh, in_specs=in_specs, out_specs=out_specs, check_vma=False
    )
```

profile of v0, /device:TPU:1, one launch (start us, length us, event | category | flops | bytes accessed | tf_op | source)
XLA Modules:
  0.0 594.3 jit_solution(12511385148093484768)
XLA Ops:
  12.5 26.5 %all-gather = bf16[8,1,512]{2,1,0:T(2,128)(2,1)S(1)} all-gather(bf16[1,1,512]{2,1,0:T(2,128)(2,1)S(1)} %reshape.227), channel_id=1, replica_groups=mesh['row'=8,'col'=32] {'row'}, dimensions={0}, use_global_device_ids=true | all-gather | bytes 9216 | tf_op jit(solution)/shard_map/all_gather | solution.py:27
  40.8 39.4 %all-gather.6.cloned.1.call-done = bf16[2,1,4096,128]{2,3,1,0:T(8,128)(2,1)} async-done(((bf16[2,1,128,128]{2,3,1,0:T(8,128)(2,1)}), bf16[2,1,4096,128]{2,3,1,0:T(8,128)(2,1)}) %all-gather.6.cloned.1.call-update) | async-done | bytes 2097168 | tf_op jit(solution)/shard_map/all_gather | solution.py:43
  81.9 75.9 %all-gather.4.cloned.1.call-done = bf16[4,128,4096]{1,2,0:T(8,128)(2,1)} async-done(((bf16[4,128,512]{1,2,0:T(8,128)(2,1)}), bf16[4,128,4096]{1,2,0:T(8,128)(2,1)}) %all-gather.4.cloned.1.call-update) | async-done | bytes 4194320 | tf_op jit(solution)/shard_map/all_gather | solution.py:26
  165.5 3.7 fusion.20
  169.2 4.3 broadcast_in_dim.39
  173.5 292.2 %while.22 = (s32[]{:T(128)}, bf16[2,1,128,128]{2,3,1,0:T(8,128)(2,1)S(1)}, f32[2,1,128,128]{2,3,1,0:T(8,128)S(1)}, f32[1,128,4,32]{1,3,2,0:T(8,128)S(1)}, f32[4,...) while((s32[]{:T(128)}, ...), condition=%wide.region_4.5_spmd.clone, body=%wide.region_3.4_spmd.clone.sunk | while | flops 21594132 | bytes 4035002 | solution.py:101
  209.1 3.3 collective-permute-done
  212.4 2.9 collective-permute-done.1
  218.2 3.5 collective-permute-done
  221.7 2.9 collective-permute-done.1
  227.6 3.4 collective-permute-done
  231.0 2.9 collective-permute-done.1
  236.9 3.4 collective-permute-done
  240.3 2.9 collective-permute-done.1
  246.1 3.5 collective-permute-done
  255.4 3.5 collective-permute-done
  264.6 3.5 collective-permute-done
  268.1 2.9 collective-permute-done.1
  273.9 3.5 collective-permute-done
  277.4 2.9 collective-permute-done.1
  283.2 3.4 collective-permute-done
  286.7 2.9 collective-permute-done.1
  292.5 3.4 collective-permute-done
  301.7 3.5 collective-permute-done
  305.2 2.9 collective-permute-done.1
  311.0 3.4 collective-permute-done
  314.5 2.9 collective-permute-done.1
  320.4 3.4 collective-permute-done
  329.6 3.5 collective-permute-done
  333.0 2.9 collective-permute-done.1
  338.9 3.4 collective-permute-done
  342.4 2.9 collective-permute-done.1
  348.2 3.5 collective-permute-done
  357.4 3.5 collective-permute-done
  360.9 2.9 collective-permute-done.1
  366.8 3.4 collective-permute-done
  376.0 3.5 collective-permute-done
  385.3 3.5 collective-permute-done
  394.5 3.5 collective-permute-done
  403.8 3.5 collective-permute-done
  413.0 3.5 collective-permute-done
  416.5 2.9 collective-permute-done.1
  422.3 3.5 collective-permute-done
  431.6 3.5 collective-permute-done
  440.8 3.5 collective-permute-done
  450.1 3.5 collective-permute-done
  459.4 3.5 collective-permute-done
  467.2 120.6 %reduce-scatter.2.cloned.1.call-done = f32[4,128,512]{2,1,0:T(8,128)} async-done(((f32[4,128,4096]{2,1,0:T(8,128)}), f32[4,128,512]{2,1,0:T(8,128)}) %reduce-scatter.2.cloned.1.call-update) | async-done | bytes 1048592 | tf_op jit(solution)/shard_map/reduce_scatter | solution.py:107
  (439 shorter events, 173.4 us)
Async XLA Ops:
  7.2 73.1 %all-gather.6.cloned.1.call-start = ((), (), s32[]{:S(2)}) async-start(), calls=%async_computation.2 | async-start | bytes 2162688 | tf_op jit(solution)/shard_map/all_gather | solution.py:43
  9.6 148.2 %all-gather.4.cloned.1.call-start = ((), (), s32[]{:S(2)}) async-start(), calls=%async_computation.1 | async-start | bytes 4718592 | tf_op jit(solution)/shard_map/all_gather | solution.py:26
  11.7 576.1 %reduce-scatter.2.cloned.1.call-start = ((), (), s32[]{:S(2)}) async-start(), calls=%async_computation.3 | async-start | bytes 9437184 | tf_op jit(solution)/shard_map/reduce_scatter | solution.py:107
  187.5 6.4 %collective-permute-start = (bf16[2,1,128,128]{2,3,1,0:T(8,128)(2,1)S(1)}, bf16[2,1,128,128]{2,3,1,0:T(8,128)(2,1)S(1)}, u32[]{:S(2)}, u32[]{:S(2)}) collective-permute-start(bf16[2,1,128,128]{2,3,1,0:T(8,128)(2,1)S(1)} %copy.55), channel_id=1, source_target_pairs={{0,1},{1,2},{2,3},{3,4},{4,5},{5,6},{6,7},{7,8},{8,9},{9,10},{10,1... | collective-permute-start | bytes 196616 | tf_op jit(solution)/shard_map/while/body/eval_jaxpr/ppermute | solution.py:15
  196.8 6.4 %collective-permute-start = (bf16[2,1,128,128]{2,3,1,0:T(8,128)(2,1)S(1)}, bf16[2,1,128,128]{2,3,1,0:T(8,128)(2,1)S(1)}, u32[]{:S(2)}, u32[]{:S(2)}) collective-permute-start(bf16[2,1,128,128]{2,3,1,0:T(8,128)(2,1)S(1)} %copy.55), channel_id=1, source_target_pairs={{0,1},{1,2},{2,3},{3,4},{4,5},{5,6},{6,7},{7,8},{8,9},{9,10},{10,1... | collective-permute-start | bytes 196616 | tf_op jit(solution)/shard_map/while/body/eval_jaxpr/ppermute | solution.py:15
  206.0 6.4 %collective-permute-start = (bf16[2,1,128,128]{2,3,1,0:T(8,128)(2,1)S(1)}, bf16[2,1,128,128]{2,3,1,0:T(8,128)(2,1)S(1)}, u32[]{:S(2)}, u32[]{:S(2)}) collective-permute-start(bf16[2,1,128,128]{2,3,1,0:T(8,128)(2,1)S(1)} %copy.55), channel_id=1, source_target_pairs={{0,1},{1,2},{2,3},{3,4},{4,5},{5,6},{6,7},{7,8},{8,9},{9,10},{10,1... | collective-permute-start | bytes 196616 | tf_op jit(solution)/shard_map/while/body/eval_jaxpr/ppermute | solution.py:15
  208.7 6.6 %collective-permute-start.1 = (f32[2,1,128,128]{2,3,1,0:T(8,128)S(1)}, f32[2,1,128,128]{2,3,1,0:T(8,128)S(1)}, u32[]{:S(2)}, u32[]{:S(2)}) collective-permute-start(f32[2,1,128,128]{2,3,1,0:T(8,128)S(1)} %maximum_add_fusion.2), channel_id=1, source_target_pairs={{0,1},{1,2},{2,3},{3,4},{4,5},{5,6},{6,7},{7,8},{8,9},{9,10},{10,1... | collective-permute-start | bytes 393224 | tf_op jit(solution)/shard_map/while/body/eval_jaxpr/ppermute | solution.py:15
  215.3 6.4 %collective-permute-start = (bf16[2,1,128,128]{2,3,1,0:T(8,128)(2,1)S(1)}, bf16[2,1,128,128]{2,3,1,0:T(8,128)(2,1)S(1)}, u32[]{:S(2)}, u32[]{:S(2)}) collective-permute-start(bf16[2,1,128,128]{2,3,1,0:T(8,128)(2,1)S(1)} %copy.55), channel_id=1, source_target_pairs={{0,1},{1,2},{2,3},{3,4},{4,5},{5,6},{6,7},{7,8},{8,9},{9,10},{10,1... | collective-permute-start | bytes 196616 | tf_op jit(solution)/shard_map/while/body/eval_jaxpr/ppermute | solution.py:15
  218.0 6.6 %collective-permute-start.1 = (f32[2,1,128,128]{2,3,1,0:T(8,128)S(1)}, f32[2,1,128,128]{2,3,1,0:T(8,128)S(1)}, u32[]{:S(2)}, u32[]{:S(2)}) collective-permute-start(f32[2,1,128,128]{2,3,1,0:T(8,128)S(1)} %maximum_add_fusion.2), channel_id=1, source_target_pairs={{0,1},{1,2},{2,3},{3,4},{4,5},{5,6},{6,7},{7,8},{8,9},{9,10},{10,1... | collective-permute-start | bytes 393224 | tf_op jit(solution)/shard_map/while/body/eval_jaxpr/ppermute | solution.py:15
  224.6 6.4 %collective-permute-start = (bf16[2,1,128,128]{2,3,1,0:T(8,128)(2,1)S(1)}, bf16[2,1,128,128]{2,3,1,0:T(8,128)(2,1)S(1)}, u32[]{:S(2)}, u32[]{:S(2)}) collective-permute-start(bf16[2,1,128,128]{2,3,1,0:T(8,128)(2,1)S(1)} %copy.55), channel_id=1, source_target_pairs={{0,1},{1,2},{2,3},{3,4},{4,5},{5,6},{6,7},{7,8},{8,9},{9,10},{10,1... | collective-permute-start | bytes 196616 | tf_op jit(solution)/shard_map/while/body/eval_jaxpr/ppermute | solution.py:15
  227.3 6.6 %collective-permute-start.1 = (f32[2,1,128,128]{2,3,1,0:T(8,128)S(1)}, f32[2,1,128,128]{2,3,1,0:T(8,128)S(1)}, u32[]{:S(2)}, u32[]{:S(2)}) collective-permute-start(f32[2,1,128,128]{2,3,1,0:T(8,128)S(1)} %maximum_add_fusion.2), channel_id=1, source_target_pairs={{0,1},{1,2},{2,3},{3,4},{4,5},{5,6},{6,7},{7,8},{8,9},{9,10},{10,1... | collective-permute-start | bytes 393224 | tf_op jit(solution)/shard_map/while/body/eval_jaxpr/ppermute | solution.py:15
  233.9 6.4 %collective-permute-start = (bf16[2,1,128,128]{2,3,1,0:T(8,128)(2,1)S(1)}, bf16[2,1,128,128]{2,3,1,0:T(8,128)(2,1)S(1)}, u32[]{:S(2)}, u32[]{:S(2)}) collective-permute-start(bf16[2,1,128,128]{2,3,1,0:T(8,128)(2,1)S(1)} %copy.55), channel_id=1, source_target_pairs={{0,1},{1,2},{2,3},{3,4},{4,5},{5,6},{6,7},{7,8},{8,9},{9,10},{10,1... | collective-permute-start | bytes 196616 | tf_op jit(solution)/shard_map/while/body/eval_jaxpr/ppermute | solution.py:15
  236.6 6.6 %collective-permute-start.1 = (f32[2,1,128,128]{2,3,1,0:T(8,128)S(1)}, f32[2,1,128,128]{2,3,1,0:T(8,128)S(1)}, u32[]{:S(2)}, u32[]{:S(2)}) collective-permute-start(f32[2,1,128,128]{2,3,1,0:T(8,128)S(1)} %maximum_add_fusion.2), channel_id=1, source_target_pairs={{0,1},{1,2},{2,3},{3,4},{4,5},{5,6},{6,7},{7,8},{8,9},{9,10},{10,1... | collective-permute-start | bytes 393224 | tf_op jit(solution)/shard_map/while/body/eval_jaxpr/ppermute | solution.py:15
  243.2 6.4 %collective-permute-start = (bf16[2,1,128,128]{2,3,1,0:T(8,128)(2,1)S(1)}, bf16[2,1,128,128]{2,3,1,0:T(8,128)(2,1)S(1)}, u32[]{:S(2)}, u32[]{:S(2)}) collective-permute-start(bf16[2,1,128,128]{2,3,1,0:T(8,128)(2,1)S(1)} %copy.55), channel_id=1, source_target_pairs={{0,1},{1,2},{2,3},{3,4},{4,5},{5,6},{6,7},{7,8},{8,9},{9,10},{10,1... | collective-permute-start | bytes 196616 | tf_op jit(solution)/shard_map/while/body/eval_jaxpr/ppermute | solution.py:15
  245.8 6.6 %collective-permute-start.1 = (f32[2,1,128,128]{2,3,1,0:T(8,128)S(1)}, f32[2,1,128,128]{2,3,1,0:T(8,128)S(1)}, u32[]{:S(2)}, u32[]{:S(2)}) collective-permute-start(f32[2,1,128,128]{2,3,1,0:T(8,128)S(1)} %maximum_add_fusion.2), channel_id=1, source_target_pairs={{0,1},{1,2},{2,3},{3,4},{4,5},{5,6},{6,7},{7,8},{8,9},{9,10},{10,1... | collective-permute-start | bytes 393224 | tf_op jit(solution)/shard_map/while/body/eval_jaxpr/ppermute | solution.py:15
  252.4 6.4 %collective-permute-start = (bf16[2,1,128,128]{2,3,1,0:T(8,128)(2,1)S(1)}, bf16[2,1,128,128]{2,3,1,0:T(8,128)(2,1)S(1)}, u32[]{:S(2)}, u32[]{:S(2)}) collective-permute-start(bf16[2,1,128,128]{2,3,1,0:T(8,128)(2,1)S(1)} %copy.55), channel_id=1, source_target_pairs={{0,1},{1,2},{2,3},{3,4},{4,5},{5,6},{6,7},{7,8},{8,9},{9,10},{10,1... | collective-permute-start | bytes 196616 | tf_op jit(solution)/shard_map/while/body/eval_jaxpr/ppermute | solution.py:15
  255.1 6.6 %collective-permute-start.1 = (f32[2,1,128,128]{2,3,1,0:T(8,128)S(1)}, f32[2,1,128,128]{2,3,1,0:T(8,128)S(1)}, u32[]{:S(2)}, u32[]{:S(2)}) collective-permute-start(f32[2,1,128,128]{2,3,1,0:T(8,128)S(1)} %maximum_add_fusion.2), channel_id=1, source_target_pairs={{0,1},{1,2},{2,3},{3,4},{4,5},{5,6},{6,7},{7,8},{8,9},{9,10},{10,1... | collective-permute-start | bytes 393224 | tf_op jit(solution)/shard_map/while/body/eval_jaxpr/ppermute | solution.py:15
  261.7 6.4 %collective-permute-start = (bf16[2,1,128,128]{2,3,1,0:T(8,128)(2,1)S(1)}, bf16[2,1,128,128]{2,3,1,0:T(8,128)(2,1)S(1)}, u32[]{:S(2)}, u32[]{:S(2)}) collective-permute-start(bf16[2,1,128,128]{2,3,1,0:T(8,128)(2,1)S(1)} %copy.55), channel_id=1, source_target_pairs={{0,1},{1,2},{2,3},{3,4},{4,5},{5,6},{6,7},{7,8},{8,9},{9,10},{10,1... | collective-permute-start | bytes 196616 | tf_op jit(solution)/shard_map/while/body/eval_jaxpr/ppermute | solution.py:15
  264.4 6.6 %collective-permute-start.1 = (f32[2,1,128,128]{2,3,1,0:T(8,128)S(1)}, f32[2,1,128,128]{2,3,1,0:T(8,128)S(1)}, u32[]{:S(2)}, u32[]{:S(2)}) collective-permute-start(f32[2,1,128,128]{2,3,1,0:T(8,128)S(1)} %maximum_add_fusion.2), channel_id=1, source_target_pairs={{0,1},{1,2},{2,3},{3,4},{4,5},{5,6},{6,7},{7,8},{8,9},{9,10},{10,1... | collective-permute-start | bytes 393224 | tf_op jit(solution)/shard_map/while/body/eval_jaxpr/ppermute | solution.py:15
  273.7 6.6 %collective-permute-start.1 = (f32[2,1,128,128]{2,3,1,0:T(8,128)S(1)}, f32[2,1,128,128]{2,3,1,0:T(8,128)S(1)}, u32[]{:S(2)}, u32[]{:S(2)}) collective-permute-start(f32[2,1,128,128]{2,3,1,0:T(8,128)S(1)} %maximum_add_fusion.2), channel_id=1, source_target_pairs={{0,1},{1,2},{2,3},{3,4},{4,5},{5,6},{6,7},{7,8},{8,9},{9,10},{10,1... | collective-permute-start | bytes 393224 | tf_op jit(solution)/shard_map/while/body/eval_jaxpr/ppermute | solution.py:15
  280.2 6.4 %collective-permute-start = (bf16[2,1,128,128]{2,3,1,0:T(8,128)(2,1)S(1)}, bf16[2,1,128,128]{2,3,1,0:T(8,128)(2,1)S(1)}, u32[]{:S(2)}, u32[]{:S(2)}) collective-permute-start(bf16[2,1,128,128]{2,3,1,0:T(8,128)(2,1)S(1)} %copy.55), channel_id=1, source_target_pairs={{0,1},{1,2},{2,3},{3,4},{4,5},{5,6},{6,7},{7,8},{8,9},{9,10},{10,1... | collective-permute-start | bytes 196616 | tf_op jit(solution)/shard_map/while/body/eval_jaxpr/ppermute | solution.py:15
  282.9 6.6 %collective-permute-start.1 = (f32[2,1,128,128]{2,3,1,0:T(8,128)S(1)}, f32[2,1,128,128]{2,3,1,0:T(8,128)S(1)}, u32[]{:S(2)}, u32[]{:S(2)}) collective-permute-start(f32[2,1,128,128]{2,3,1,0:T(8,128)S(1)} %maximum_add_fusion.2), channel_id=1, source_target_pairs={{0,1},{1,2},{2,3},{3,4},{4,5},{5,6},{6,7},{7,8},{8,9},{9,10},{10,1... | collective-permute-start | bytes 393224 | tf_op jit(solution)/shard_map/while/body/eval_jaxpr/ppermute | solution.py:15
  289.5 6.4 %collective-permute-start = (bf16[2,1,128,128]{2,3,1,0:T(8,128)(2,1)S(1)}, bf16[2,1,128,128]{2,3,1,0:T(8,128)(2,1)S(1)}, u32[]{:S(2)}, u32[]{:S(2)}) collective-permute-start(bf16[2,1,128,128]{2,3,1,0:T(8,128)(2,1)S(1)} %copy.55), channel_id=1, source_target_pairs={{0,1},{1,2},{2,3},{3,4},{4,5},{5,6},{6,7},{7,8},{8,9},{9,10},{10,1... | collective-permute-start | bytes 196616 | tf_op jit(solution)/shard_map/while/body/eval_jaxpr/ppermute | solution.py:15
  292.2 6.5 %collective-permute-start.1 = (f32[2,1,128,128]{2,3,1,0:T(8,128)S(1)}, f32[2,1,128,128]{2,3,1,0:T(8,128)S(1)}, u32[]{:S(2)}, u32[]{:S(2)}) collective-permute-start(f32[2,1,128,128]{2,3,1,0:T(8,128)S(1)} %maximum_add_fusion.2), channel_id=1, source_target_pairs={{0,1},{1,2},{2,3},{3,4},{4,5},{5,6},{6,7},{7,8},{8,9},{9,10},{10,1... | collective-permute-start | bytes 393224 | tf_op jit(solution)/shard_map/while/body/eval_jaxpr/ppermute | solution.py:15
  298.8 6.4 %collective-permute-start = (bf16[2,1,128,128]{2,3,1,0:T(8,128)(2,1)S(1)}, bf16[2,1,128,128]{2,3,1,0:T(8,128)(2,1)S(1)}, u32[]{:S(2)}, u32[]{:S(2)}) collective-permute-start(bf16[2,1,128,128]{2,3,1,0:T(8,128)(2,1)S(1)} %copy.55), channel_id=1, source_target_pairs={{0,1},{1,2},{2,3},{3,4},{4,5},{5,6},{6,7},{7,8},{8,9},{9,10},{10,1... | collective-permute-start | bytes 196616 | tf_op jit(solution)/shard_map/while/body/eval_jaxpr/ppermute | solution.py:15
  301.4 6.6 %collective-permute-start.1 = (f32[2,1,128,128]{2,3,1,0:T(8,128)S(1)}, f32[2,1,128,128]{2,3,1,0:T(8,128)S(1)}, u32[]{:S(2)}, u32[]{:S(2)}) collective-permute-start(f32[2,1,128,128]{2,3,1,0:T(8,128)S(1)} %maximum_add_fusion.2), channel_id=1, source_target_pairs={{0,1},{1,2},{2,3},{3,4},{4,5},{5,6},{6,7},{7,8},{8,9},{9,10},{10,1... | collective-permute-start | bytes 393224 | tf_op jit(solution)/shard_map/while/body/eval_jaxpr/ppermute | solution.py:15
  308.1 6.4 %collective-permute-start = (bf16[2,1,128,128]{2,3,1,0:T(8,128)(2,1)S(1)}, bf16[2,1,128,128]{2,3,1,0:T(8,128)(2,1)S(1)}, u32[]{:S(2)}, u32[]{:S(2)}) collective-permute-start(bf16[2,1,128,128]{2,3,1,0:T(8,128)(2,1)S(1)} %copy.55), channel_id=1, source_target_pairs={{0,1},{1,2},{2,3},{3,4},{4,5},{5,6},{6,7},{7,8},{8,9},{9,10},{10,1... | collective-permute-start | bytes 196616 | tf_op jit(solution)/shard_map/while/body/eval_jaxpr/ppermute | solution.py:15
  310.8 6.6 %collective-permute-start.1 = (f32[2,1,128,128]{2,3,1,0:T(8,128)S(1)}, f32[2,1,128,128]{2,3,1,0:T(8,128)S(1)}, u32[]{:S(2)}, u32[]{:S(2)}) collective-permute-start(f32[2,1,128,128]{2,3,1,0:T(8,128)S(1)} %maximum_add_fusion.2), channel_id=1, source_target_pairs={{0,1},{1,2},{2,3},{3,4},{4,5},{5,6},{6,7},{7,8},{8,9},{9,10},{10,1... | collective-permute-start | bytes 393224 | tf_op jit(solution)/shard_map/while/body/eval_jaxpr/ppermute | solution.py:15
  317.4 6.4 %collective-permute-start = (bf16[2,1,128,128]{2,3,1,0:T(8,128)(2,1)S(1)}, bf16[2,1,128,128]{2,3,1,0:T(8,128)(2,1)S(1)}, u32[]{:S(2)}, u32[]{:S(2)}) collective-permute-start(bf16[2,1,128,128]{2,3,1,0:T(8,128)(2,1)S(1)} %copy.55), channel_id=1, source_target_pairs={{0,1},{1,2},{2,3},{3,4},{4,5},{5,6},{6,7},{7,8},{8,9},{9,10},{10,1... | collective-permute-start | bytes 196616 | tf_op jit(solution)/shard_map/while/body/eval_jaxpr/ppermute | solution.py:15
  320.1 6.5 %collective-permute-start.1 = (f32[2,1,128,128]{2,3,1,0:T(8,128)S(1)}, f32[2,1,128,128]{2,3,1,0:T(8,128)S(1)}, u32[]{:S(2)}, u32[]{:S(2)}) collective-permute-start(f32[2,1,128,128]{2,3,1,0:T(8,128)S(1)} %maximum_add_fusion.2), channel_id=1, source_target_pairs={{0,1},{1,2},{2,3},{3,4},{4,5},{5,6},{6,7},{7,8},{8,9},{9,10},{10,1... | collective-permute-start | bytes 393224 | tf_op jit(solution)/shard_map/while/body/eval_jaxpr/ppermute | solution.py:15
  326.6 6.4 %collective-permute-start = (bf16[2,1,128,128]{2,3,1,0:T(8,128)(2,1)S(1)}, bf16[2,1,128,128]{2,3,1,0:T(8,128)(2,1)S(1)}, u32[]{:S(2)}, u32[]{:S(2)}) collective-permute-start(bf16[2,1,128,128]{2,3,1,0:T(8,128)(2,1)S(1)} %copy.55), channel_id=1, source_target_pairs={{0,1},{1,2},{2,3},{3,4},{4,5},{5,6},{6,7},{7,8},{8,9},{9,10},{10,1... | collective-permute-start | bytes 196616 | tf_op jit(solution)/shard_map/while/body/eval_jaxpr/ppermute | solution.py:15
  329.3 6.6 %collective-permute-start.1 = (f32[2,1,128,128]{2,3,1,0:T(8,128)S(1)}, f32[2,1,128,128]{2,3,1,0:T(8,128)S(1)}, u32[]{:S(2)}, u32[]{:S(2)}) collective-permute-start(f32[2,1,128,128]{2,3,1,0:T(8,128)S(1)} %maximum_add_fusion.2), channel_id=1, source_target_pairs={{0,1},{1,2},{2,3},{3,4},{4,5},{5,6},{6,7},{7,8},{8,9},{9,10},{10,1... | collective-permute-start | bytes 393224 | tf_op jit(solution)/shard_map/while/body/eval_jaxpr/ppermute | solution.py:15
  335.9 6.4 %collective-permute-start = (bf16[2,1,128,128]{2,3,1,0:T(8,128)(2,1)S(1)}, bf16[2,1,128,128]{2,3,1,0:T(8,128)(2,1)S(1)}, u32[]{:S(2)}, u32[]{:S(2)}) collective-permute-start(bf16[2,1,128,128]{2,3,1,0:T(8,128)(2,1)S(1)} %copy.55), channel_id=1, source_target_pairs={{0,1},{1,2},{2,3},{3,4},{4,5},{5,6},{6,7},{7,8},{8,9},{9,10},{10,1... | collective-permute-start | bytes 196616 | tf_op jit(solution)/shard_map/while/body/eval_jaxpr/ppermute | solution.py:15
  338.7 6.5 %collective-permute-start.1 = (f32[2,1,128,128]{2,3,1,0:T(8,128)S(1)}, f32[2,1,128,128]{2,3,1,0:T(8,128)S(1)}, u32[]{:S(2)}, u32[]{:S(2)}) collective-permute-start(f32[2,1,128,128]{2,3,1,0:T(8,128)S(1)} %maximum_add_fusion.2), channel_id=1, source_target_pairs={{0,1},{1,2},{2,3},{3,4},{4,5},{5,6},{6,7},{7,8},{8,9},{9,10},{10,1... | collective-permute-start | bytes 393224 | tf_op jit(solution)/shard_map/while/body/eval_jaxpr/ppermute | solution.py:15
  345.2 6.4 %collective-permute-start = (bf16[2,1,128,128]{2,3,1,0:T(8,128)(2,1)S(1)}, bf16[2,1,128,128]{2,3,1,0:T(8,128)(2,1)S(1)}, u32[]{:S(2)}, u32[]{:S(2)}) collective-permute-start(bf16[2,1,128,128]{2,3,1,0:T(8,128)(2,1)S(1)} %copy.55), channel_id=1, source_target_pairs={{0,1},{1,2},{2,3},{3,4},{4,5},{5,6},{6,7},{7,8},{8,9},{9,10},{10,1... | collective-permute-start | bytes 196616 | tf_op jit(solution)/shard_map/while/body/eval_jaxpr/ppermute | solution.py:15
  347.9 6.6 %collective-permute-start.1 = (f32[2,1,128,128]{2,3,1,0:T(8,128)S(1)}, f32[2,1,128,128]{2,3,1,0:T(8,128)S(1)}, u32[]{:S(2)}, u32[]{:S(2)}) collective-permute-start(f32[2,1,128,128]{2,3,1,0:T(8,128)S(1)} %maximum_add_fusion.2), channel_id=1, source_target_pairs={{0,1},{1,2},{2,3},{3,4},{4,5},{5,6},{6,7},{7,8},{8,9},{9,10},{10,1... | collective-permute-start | bytes 393224 | tf_op jit(solution)/shard_map/while/body/eval_jaxpr/ppermute | solution.py:15
  357.1 6.6 %collective-permute-start.1 = (f32[2,1,128,128]{2,3,1,0:T(8,128)S(1)}, f32[2,1,128,128]{2,3,1,0:T(8,128)S(1)}, u32[]{:S(2)}, u32[]{:S(2)}) collective-permute-start(f32[2,1,128,128]{2,3,1,0:T(8,128)S(1)} %maximum_add_fusion.2), channel_id=1, source_target_pairs={{0,1},{1,2},{2,3},{3,4},{4,5},{5,6},{6,7},{7,8},{8,9},{9,10},{10,1... | collective-permute-start | bytes 393224 | tf_op jit(solution)/shard_map/while/body/eval_jaxpr/ppermute | solution.py:15
  366.5 6.5 %collective-permute-start.1 = (f32[2,1,128,128]{2,3,1,0:T(8,128)S(1)}, f32[2,1,128,128]{2,3,1,0:T(8,128)S(1)}, u32[]{:S(2)}, u32[]{:S(2)}) collective-permute-start(f32[2,1,128,128]{2,3,1,0:T(8,128)S(1)} %maximum_add_fusion.2), channel_id=1, source_target_pairs={{0,1},{1,2},{2,3},{3,4},{4,5},{5,6},{6,7},{7,8},{8,9},{9,10},{10,1... | collective-permute-start | bytes 393224 | tf_op jit(solution)/shard_map/while/body/eval_jaxpr/ppermute | solution.py:15
  375.7 6.6 %collective-permute-start.1 = (f32[2,1,128,128]{2,3,1,0:T(8,128)S(1)}, f32[2,1,128,128]{2,3,1,0:T(8,128)S(1)}, u32[]{:S(2)}, u32[]{:S(2)}) collective-permute-start(f32[2,1,128,128]{2,3,1,0:T(8,128)S(1)} %maximum_add_fusion.2), channel_id=1, source_target_pairs={{0,1},{1,2},{2,3},{3,4},{4,5},{5,6},{6,7},{7,8},{8,9},{9,10},{10,1... | collective-permute-start | bytes 393224 | tf_op jit(solution)/shard_map/while/body/eval_jaxpr/ppermute | solution.py:15
  385.0 6.6 %collective-permute-start.1 = (f32[2,1,128,128]{2,3,1,0:T(8,128)S(1)}, f32[2,1,128,128]{2,3,1,0:T(8,128)S(1)}, u32[]{:S(2)}, u32[]{:S(2)}) collective-permute-start(f32[2,1,128,128]{2,3,1,0:T(8,128)S(1)} %maximum_add_fusion.2), channel_id=1, source_target_pairs={{0,1},{1,2},{2,3},{3,4},{4,5},{5,6},{6,7},{7,8},{8,9},{9,10},{10,1... | collective-permute-start | bytes 393224 | tf_op jit(solution)/shard_map/while/body/eval_jaxpr/ppermute | solution.py:15
  394.2 6.6 %collective-permute-start.1 = (f32[2,1,128,128]{2,3,1,0:T(8,128)S(1)}, f32[2,1,128,128]{2,3,1,0:T(8,128)S(1)}, u32[]{:S(2)}, u32[]{:S(2)}) collective-permute-start(f32[2,1,128,128]{2,3,1,0:T(8,128)S(1)} %maximum_add_fusion.2), channel_id=1, source_target_pairs={{0,1},{1,2},{2,3},{3,4},{4,5},{5,6},{6,7},{7,8},{8,9},{9,10},{10,1... | collective-permute-start | bytes 393224 | tf_op jit(solution)/shard_map/while/body/eval_jaxpr/ppermute | solution.py:15
  403.5 6.6 %collective-permute-start.1 = (f32[2,1,128,128]{2,3,1,0:T(8,128)S(1)}, f32[2,1,128,128]{2,3,1,0:T(8,128)S(1)}, u32[]{:S(2)}, u32[]{:S(2)}) collective-permute-start(f32[2,1,128,128]{2,3,1,0:T(8,128)S(1)} %maximum_add_fusion.2), channel_id=1, source_target_pairs={{0,1},{1,2},{2,3},{3,4},{4,5},{5,6},{6,7},{7,8},{8,9},{9,10},{10,1... | collective-permute-start | bytes 393224 | tf_op jit(solution)/shard_map/while/body/eval_jaxpr/ppermute | solution.py:15
  412.8 6.6 %collective-permute-start.1 = (f32[2,1,128,128]{2,3,1,0:T(8,128)S(1)}, f32[2,1,128,128]{2,3,1,0:T(8,128)S(1)}, u32[]{:S(2)}, u32[]{:S(2)}) collective-permute-start(f32[2,1,128,128]{2,3,1,0:T(8,128)S(1)} %maximum_add_fusion.2), channel_id=1, source_target_pairs={{0,1},{1,2},{2,3},{3,4},{4,5},{5,6},{6,7},{7,8},{8,9},{9,10},{10,1... | collective-permute-start | bytes 393224 | tf_op jit(solution)/shard_map/while/body/eval_jaxpr/ppermute | solution.py:15
  422.1 6.6 %collective-permute-start.1 = (f32[2,1,128,128]{2,3,1,0:T(8,128)S(1)}, f32[2,1,128,128]{2,3,1,0:T(8,128)S(1)}, u32[]{:S(2)}, u32[]{:S(2)}) collective-permute-start(f32[2,1,128,128]{2,3,1,0:T(8,128)S(1)} %maximum_add_fusion.2), channel_id=1, source_target_pairs={{0,1},{1,2},{2,3},{3,4},{4,5},{5,6},{6,7},{7,8},{8,9},{9,10},{10,1... | collective-permute-start | bytes 393224 | tf_op jit(solution)/shard_map/while/body/eval_jaxpr/ppermute | solution.py:15
  431.3 6.6 %collective-permute-start.1 = (f32[2,1,128,128]{2,3,1,0:T(8,128)S(1)}, f32[2,1,128,128]{2,3,1,0:T(8,128)S(1)}, u32[]{:S(2)}, u32[]{:S(2)}) collective-permute-start(f32[2,1,128,128]{2,3,1,0:T(8,128)S(1)} %maximum_add_fusion.2), channel_id=1, source_target_pairs={{0,1},{1,2},{2,3},{3,4},{4,5},{5,6},{6,7},{7,8},{8,9},{9,10},{10,1... | collective-permute-start | bytes 393224 | tf_op jit(solution)/shard_map/while/body/eval_jaxpr/ppermute | solution.py:15
  440.6 6.6 %collective-permute-start.1 = (f32[2,1,128,128]{2,3,1,0:T(8,128)S(1)}, f32[2,1,128,128]{2,3,1,0:T(8,128)S(1)}, u32[]{:S(2)}, u32[]{:S(2)}) collective-permute-start(f32[2,1,128,128]{2,3,1,0:T(8,128)S(1)} %maximum_add_fusion.2), channel_id=1, source_target_pairs={{0,1},{1,2},{2,3},{3,4},{4,5},{5,6},{6,7},{7,8},{8,9},{9,10},{10,1... | collective-permute-start | bytes 393224 | tf_op jit(solution)/shard_map/while/body/eval_jaxpr/ppermute | solution.py:15
  449.8 6.6 %collective-permute-start.1 = (f32[2,1,128,128]{2,3,1,0:T(8,128)S(1)}, f32[2,1,128,128]{2,3,1,0:T(8,128)S(1)}, u32[]{:S(2)}, u32[]{:S(2)}) collective-permute-start(f32[2,1,128,128]{2,3,1,0:T(8,128)S(1)} %maximum_add_fusion.2), channel_id=1, source_target_pairs={{0,1},{1,2},{2,3},{3,4},{4,5},{5,6},{6,7},{7,8},{8,9},{9,10},{10,1... | collective-permute-start | bytes 393224 | tf_op jit(solution)/shard_map/while/body/eval_jaxpr/ppermute | solution.py:15
  459.1 6.6 %collective-permute-start.1 = (f32[2,1,128,128]{2,3,1,0:T(8,128)S(1)}, f32[2,1,128,128]{2,3,1,0:T(8,128)S(1)}, u32[]{:S(2)}, u32[]{:S(2)}) collective-permute-start(f32[2,1,128,128]{2,3,1,0:T(8,128)S(1)} %maximum_add_fusion.2), channel_id=1, source_target_pairs={{0,1},{1,2},{2,3},{3,4},{4,5},{5,6},{6,7},{7,8},{8,9},{9,10},{10,1... | collective-permute-start | bytes 393224 | tf_op jit(solution)/shard_map/while/body/eval_jaxpr/ppermute | solution.py:15
  (21 other events, 119.0 us)
Sparse Core Ops, SparseCore 0:
  10.3 69.8 all-gather.5
  83.4 74.3 all-gather.3
  465.8 121.9 reduce-scatter.1
where the time goes:
time: 595 us; the launch traced here: 594 us
  waiting for transfers between devices  426 us (72%)
  matrix products  59.9 us (10%)
  local copies, waits for them, and re-layouts  48.3 us (8%)
  blocking collectives  26.5 us (4%)
  between operations  13.9 us (2%)
  starting transfers between devices  11.1 us (2%)
  other arithmetic  6.32 us (1%)
    ppermute x64, waiting for transfers between devices, shifted(): return lax.ppermute(value, axis, pairs)  190 us
    reduce_scatter x1, waiting for transfers between devices, on_device(): lax.psum_scatter(bias_acc, 'row', scatter_dimension=2, tiled=True)  121 us
    all_gather x1, waiting for transfers between devices, on_device(): lax.all_gather(pair_bias, 'row', axis=2, tiled=True)  75.9 us
    all_gather x1, waiting for transfers between devices, on_device(): tile_kv = lax.all_gather(stacked, 'col', axis=2, tiled=True)  39.4 us
    dynamic_slice x64, local copies, waits for them, and re-layouts, scores_of(): lax.dynamic_slice_in_dim(masked_bias, offset, length, 2).astype(jnp.float32)  33.7 us
    dot_general x32, matrix products, backward_block(): jnp.einsum('rjhd,rkhd->hrjk', grad_heads, value_heads, preferred_element_...  31.2 us
    all_gather x1, blocking collectives, on_device(): lax.all_gather(residue_mask.astype(jnp.bfloat16), 'row', axis=0, tiled=True)  26.5 us
  transfers between devices with their start and end apart: 67, of which 65 were waited for; matrix products, arithmetic and copies ran while one was open for 16% of the time, Pallas kernels for 0%

commit v1 on v0

v1 whole, which is shorter than its diff:
```python
import math

import jax
import jax.numpy as jnp
from jax import lax
from jax.experimental import pallas as pl
from jax.experimental.pallas import tpu as pltpu
from jax.sharding import PartitionSpec as P

HEADS = 4
HEAD_DIM = 32
ROWS = 8
PLANES = 8
BLOCK = 128
KEYS = 512
CHANNELS = 128
MESH = pl.DeviceIdType.MESH
LOG2E = 1.4426950408889634
SCALE = 1.0 / math.sqrt(HEAD_DIM)
F32 = jnp.float32
BF16 = jnp.bfloat16
DISTANCES = (1, 7, 2, 6, 3, 5, 4)


def wait_copy(ref, sem):
    pltpu.make_async_copy(ref, ref, sem).wait()


def nt(a, b):
    return lax.dot_general(a, b, (((1,), (1,)), ((), ())), preferred_element_type=F32)


def kernel(
    q_ref, k_ref, v_ref, b_ref, m_ref, g_ref,
    dq_ref, dk_ref, dv_ref, db_ref,
    zbuf, qg, kv, qm, bias_t, db_acc, p_buf, wg_buf, local, st, coef, wl, dl,
    own, cx_out, cx_in, rr_out, rr_in, zr_out, zr_in, zown, dq_out, dq_in,
    z_s, z_r, q_s, q_r, r_s, r_r, e_s, e_r, st_s, st_r, cx_s, cx_r, rr_s, rr_r,
    zr_s, zr_r, dq_s, dq_r,
):
    r = lax.axis_index("row")
    c = lax.axis_index("col")
    z = c // 4
    yl = (c // 2) % 2
    core = c % 2
    other = (r, c + 1 - 2 * core)

    def place(row, plane, y):
        return (row, plane * 4 + y * 2 + core)

    barrier = pltpu.get_barrier_semaphore()

    def greet(target):
        pl.semaphore_signal(barrier, inc=1, device_id=target, device_id_type=MESH)

    greet(other)
    for d in range(1, PLANES):
        greet((r, (c + 4 * d) % 32))
    for d in range(ROWS):
        for y in range(2):
            if d or y:
                greet(place((r + d) % ROWS, z, (yl + y) % 2))
    zbuf[0, z] = k_ref[0]
    zbuf[1, z] = v_ref[0]
    qg[0, r] = q_ref[0]
    qg[1, r] = g_ref[0]
    pl.semaphore_wait(barrier, 23)

    def z_copy(kind, d):
        return pltpu.make_async_remote_copy(
            zbuf.at[kind, z], zbuf.at[kind, z], z_s.at[kind, d], z_r.at[kind, d],
            device_id=(r, (c + 4 * d) % 32), device_id_type=MESH)

    def q_copy(kind, d):
        return pltpu.make_async_remote_copy(
            qg.at[kind, r], qg.at[kind, r], q_s.at[kind, d], q_r.at[kind, d],
            device_id=((r + d) % ROWS, c), device_id_type=MESH)

    for kind in range(2):
        for d in DISTANCES:
            z_copy(kind, d).start()
        for d in range(1, ROWS):
            q_copy(kind, d).start()

    def r_copy(kind, plane, y):
        return pltpu.make_async_remote_copy(
            zbuf.at[kind, plane], kv.at[kind, core, r, yl],
            r_s.at[kind, plane * 2 + y], r_r.at[kind, r * 2 + yl],
            device_id=place(plane, z, y), device_id_type=MESH)

    def spread(kind, d):
        plane = (z + PLANES - d) % PLANES
        if d:
            wait_copy(zbuf.at[kind, plane], z_r.at[kind, d])
        for y in range(2):
            mine = jnp.logical_and(plane == r, y == yl)

            @pl.when(mine)
            def _():
                pltpu.make_async_copy(
                    zbuf.at[kind, plane], kv.at[kind, core, r, yl], r_r.at[kind, r * 2 + yl]
                ).start()

            @pl.when(jnp.logical_not(mine))
            def _():
                r_copy(kind, plane, y).start()

    def e_copy(kind, i):
        return pltpu.make_async_remote_copy(
            kv.at[kind, core, i], kv.at[kind, core, i], e_s.at[kind, i], e_r.at[kind, i],
            device_id=other, device_id_type=MESH)

    def share(kind, i):
        for y in range(2):
            wait_copy(kv.at[kind, core, i, y], r_r.at[kind, i * 2 + y])
        e_copy(kind, i).start()

    spread(0, 0)
    present = m_ref[...] == 1
    for h in range(HEADS):
        masked = jnp.where(present, b_ref[h].astype(F32), -1000000000.0) * LOG2E
        for part in range(4):
            q_index = (part % 2) * 2 + part // 2
            bias_t[h, part * BLOCK:(part + 1) * BLOCK, :] = jnp.transpose(
                masked[:, q_index * BLOCK:(q_index + 1) * BLOCK])
    db_acc[...] = jnp.zeros_like(db_acc)
    for d in DISTANCES:
        spread(0, d)
    spread(1, 0)
    for step in range(ROWS):
        share(0, (r + step) % ROWS)

    lanes = lax.broadcasted_iota(jnp.int32, (BLOCK, CHANNELS), 1) // HEAD_DIM

    def split_heads(kind, i):
        block = qg[kind, i]
        for h in range(HEADS):
            qm[kind, i, h * BLOCK:(h + 1) * BLOCK, :] = jnp.where(lanes == h, block, jnp.zeros_like(block))

    def score_row(i):
        @pl.when(i != r)
        def _():
            wait_copy(qg.at[0, i], q_r.at[0, (r + ROWS - i) % ROWS])
        wait_copy(kv.at[0, 1 - core, i], e_r.at[0, i])
        split_heads(0, i)
        keys = kv[0, :, i].reshape(KEYS, CHANNELS)
        for pair in range(2):
            products = nt(keys, qm[0, i, pair * 256:(pair + 1) * 256, :])
            for half in range(2):
                h = pair * 2 + half
                s = products[:, half * BLOCK:(half + 1) * BLOCK] * (SCALE * LOG2E) + bias_t[h]
                top = jnp.max(s, axis=0, keepdims=True)
                p = jnp.exp2(s - top)
                p_buf[i, h] = p
                local[i, h:h + 1, :] = top
                local[i, HEADS + h:HEADS + h + 1, :] = jnp.sum(p, axis=0, keepdims=True)

    def first(t, carried):
        score_row((r + t) % ROWS)
        return carried

    for d in DISTANCES:
        spread(1, d)
    lax.fori_loop(0, ROWS, first, 0)
    for step in range(ROWS):
        share(1, (r + step) % ROWS)

    def second(t, carried):
        i = (r + t) % ROWS

        @pl.when(i != r)
        def _():
            wait_copy(qg.at[1, i], q_r.at[1, (r + ROWS - i) % ROWS])
        wait_copy(kv.at[1, 1 - core, i], e_r.at[1, i])
        split_heads(1, i)
        values = kv[1, :, i].reshape(KEYS, CHANNELS)
        for pair in range(2):
            products = nt(values, qm[1, i, pair * 256:(pair + 1) * 256, :])
            for half in range(2):
                h = pair * 2 + half
                wg = products[:, half * BLOCK:(half + 1) * BLOCK]
                wg_buf[i, h] = wg
                total = local[i, HEADS + h:HEADS + h + 1, :]
                dot = jnp.sum(p_buf[i, h] * wg, axis=0, keepdims=True)
                st[r, i, h:h + 1, :] = local[i, h:h + 1, :] + jnp.log(total) * LOG2E
                st[r, i, HEADS + h:HEADS + h + 1, :] = dot / total
        return carried

    lax.fori_loop(0, ROWS, second, 0)

    def st_copy(d):
        return pltpu.make_async_remote_copy(
            st.at[r], st.at[r], st_s.at[d], st_r.at[d],
            device_id=((r + d) % ROWS, c), device_id_type=MESH)

    for d in range(1, ROWS):
        st_copy(d).start()
    for d in range(1, ROWS):
        wait_copy(st.at[(r + ROWS - d) % ROWS], st_r.at[d])
    parts = [st[d] for d in range(ROWS)]
    logs = [part[:, :HEADS] for part in parts]
    peak = logs[0]
    for part in logs[1:]:
        peak = jnp.maximum(peak, part)
    shares = [jnp.exp2(part - peak) for part in logs]
    norm = sum(shares[1:], shares[0])
    delta = sum(s * part[:, HEADS:] for s, part in zip(shares, parts)) / norm
    coef[:, :HEADS] = jnp.exp2(local[:, :HEADS] - peak) / norm
    coef[:, HEADS:] = delta

    def cx_copy(t):
        return pltpu.make_async_remote_copy(
            cx_out.at[t], cx_in.at[t], cx_s.at[t], cx_r.at[t],
            device_id=other, device_id_type=MESH)

    def rr_copy(t, y):
        return pltpu.make_async_remote_copy(
            rr_out.at[t, y], rr_in.at[r, yl], rr_s.at[t * 2 + y], rr_r.at[r * 2 + yl],
            device_id=place((r + 1 + t) % ROWS, z, y), device_id_type=MESH)

    def zr_copy(row):
        return pltpu.make_async_remote_copy(
            zr_out.at[row], zr_in.at[z], zr_s.at[row], zr_r.at[z],
            device_id=(r, row * 4 + c % 4), device_id_type=MESH)

    def dq_copy(t):
        return pltpu.make_async_remote_copy(
            dq_out.at[t], dq_in.at[r], dq_s.at[t], dq_r.at[r],
            device_id=((r + 1 + t) % ROWS, c), device_id_type=MESH)

    def grads(t):
        i = (r + 1 + t) % ROWS
        keys = kv[0, :, i].reshape(KEYS, CHANNELS)
        for h in range(HEADS):
            w = p_buf[i, h] * coef[i, h:h + 1, :]
            ds = w * (wg_buf[i, h] - coef[i, HEADS + h:HEADS + h + 1, :])
            db_acc[h] += ds
            wl[:, h * BLOCK:(h + 1) * BLOCK] = w.astype(BF16)
            dl[:, h * BLOCK:(h + 1) * BLOCK] = ds.astype(BF16)
        for kind, grid in ((0, dl), (1, wl)):
            part = jnp.dot(grid[...], qm[kind, i], preferred_element_type=F32)
            part = part.reshape(2, 2, BLOCK, CHANNELS)
            for y in range(2):
                own[t, y, kind] = jnp.where(core == 0, part[0, y], part[1, y])
                cx_out[t, y, kind] = jnp.where(core == 0, part[1, y], part[0, y]).astype(BF16)
        cx_copy(t).start()
        cross = lax.dot_general(keys, dl[...], (((0,), (0,)), ((), ())), preferred_element_type=F32)
        turned = jnp.concatenate(
            [cross[h * HEAD_DIM:(h + 1) * HEAD_DIM, h * BLOCK:(h + 1) * BLOCK] for h in range(HEADS)], axis=0)
        dq_out[t] = jnp.transpose(turned).astype(BF16)

        @pl.when(i != r)
        def _():
            dq_copy(t).start()

    def merge_cores(t):
        wait_copy(cx_in.at[t], cx_r.at[t])
        for y in range(2):
            rr_out[t, y] = (own[t, y] + cx_in[t, y].astype(F32)).astype(BF16)
            mine = jnp.logical_and(t == ROWS - 1, y == yl)

            @pl.when(jnp.logical_not(mine))
            def _():
                rr_copy(t, y).start()

            @pl.when(mine)
            def _():
                pltpu.make_async_copy(rr_out.at[t, y], rr_in.at[r, yl], rr_r.at[r * 2 + yl]).start()

    def merge_pair(t):
        row = (r + 2 * ROWS - 1 - t) % ROWS
        for y in range(2):
            wait_copy(rr_in.at[row, y], rr_r.at[row * 2 + y])
        both = rr_in[row, 0].astype(F32) + rr_in[row, 1].astype(F32)

        @pl.when(row == z)
        def _():
            zown[...] = both

        @pl.when(row != z)
        def _():
            zr_out[row] = both.astype(BF16)
            zr_copy(row).start()

    lag_core, lag_pair = 1, 3

    def third(t, carried):
        @pl.when(t < ROWS)
        def _():
            grads(t)

        @pl.when(jnp.logical_and(t >= lag_core, t < ROWS + lag_core))
        def _():
            merge_cores(t - lag_core)

        @pl.when(t >= lag_pair)
        def _():
            merge_pair(t - lag_pair)
        return carried

    lax.fori_loop(0, ROWS + lag_pair, third, 0)

    for h in range(HEADS):
        for part in range(4):
            q_index = (part % 2) * 2 + part // 2
            db_ref[h, :, q_index * BLOCK:(q_index + 1) * BLOCK] = jnp.transpose(
                db_acc[h, part * BLOCK:(part + 1) * BLOCK, :])

    dq = dq_out[ROWS - 1].astype(F32)
    for d in range(1, ROWS):
        row = (r + d) % ROWS
        wait_copy(dq_in.at[row], dq_r.at[row])
        dq += dq_in[row].astype(F32)
    dq_ref[0] = dq * SCALE

    total = zown[...]
    for d in DISTANCES:
        plane = (z + PLANES - d) % PLANES
        wait_copy(zr_in.at[plane], zr_r.at[plane])
        total += zr_in[plane].astype(F32)
    dk_ref[0] = total[0] * SCALE
    dv_ref[0] = total[1]

    for kind in range(2):
        for d in range(1, 8):
            z_copy(kind, d).wait_send()
            q_copy(kind, d).wait_send()
        for plane in range(PLANES):
            for y in range(2):
                @pl.when(jnp.logical_not(jnp.logical_and(plane == r, y == yl)))
                def _():
                    r_copy(kind, plane, y).wait_send()
        for i in range(ROWS):
            e_copy(kind, i).wait_send()
    for d in range(1, ROWS):
        st_copy(d).wait_send()
    for t in range(ROWS):
        cx_copy(t).wait_send()
        for y in range(2):
            if t < ROWS - 1:
                rr_copy(t, y).wait_send()
            else:
                @pl.when(y != yl)
                def _():
                    rr_copy(t, y).wait_send()
        if t < ROWS - 1:
            dq_copy(t).wait_send()

        @pl.when(t != z)
        def _():
            zr_copy(t).wait_send()


def on_device(query_pair, key_pair, value_pair, pair_bias, residue_mask, grad_output):
    block = (BLOCK, CHANNELS)
    dma = pltpu.SemaphoreType.DMA
    scratch = [
        pltpu.VMEM((2, PLANES) + block, BF16),
        pltpu.VMEM((2, ROWS) + block, BF16),
        pltpu.VMEM((2, 2, ROWS, 2) + block, BF16),
        pltpu.VMEM((2, ROWS, HEADS * BLOCK, CHANNELS), BF16),
        pltpu.VMEM((HEADS, KEYS, BLOCK), F32),
        pltpu.VMEM((HEADS, KEYS, BLOCK), F32),
        pltpu.VMEM((ROWS, HEADS, KEYS, BLOCK), F32),
        pltpu.VMEM((ROWS, HEADS, KEYS, BLOCK), F32),
        pltpu.VMEM((ROWS, 2 * HEADS, BLOCK), F32),
        pltpu.VMEM((ROWS, ROWS, 2 * HEADS, BLOCK), F32),
        pltpu.VMEM((ROWS, 2 * HEADS, BLOCK), F32),
        pltpu.VMEM((KEYS, HEADS * BLOCK), BF16),
        pltpu.VMEM((KEYS, HEADS * BLOCK), BF16),
        pltpu.VMEM((ROWS, 2, 2) + block, F32),
        pltpu.VMEM((ROWS, 2, 2) + block, BF16),
        pltpu.VMEM((ROWS, 2, 2) + block, BF16),
        pltpu.VMEM((ROWS, 2, 2) + block, BF16),
        pltpu.VMEM((ROWS, 2, 2) + block, BF16),
        pltpu.VMEM((ROWS, 2) + block, BF16),
        pltpu.VMEM((PLANES, 2) + block, BF16),
        pltpu.VMEM((2,) + block, F32),
        pltpu.VMEM((ROWS,) + block, BF16),
        pltpu.VMEM((ROWS,) + block, BF16),
        dma((2, 8)), dma((2, 8)), dma((2, 8)), dma((2, 8)),
        dma((2, 16)), dma((2, 16)), dma((2, 8)), dma((2, 8)),
        dma((8,)), dma((8,)), dma((8,)), dma((8,)), dma((16,)), dma((16,)),
        dma((8,)), dma((8,)), dma((8,)), dma((8,)),
    ]
    vmem = pl.BlockSpec(memory_space=pltpu.VMEM)
    shape = jax.ShapeDtypeStruct
    return pl.pallas_call(
        kernel,
        out_shape=(
            shape((1,) + block, F32), shape((1,) + block, F32), shape((1,) + block, F32),
            shape((HEADS, BLOCK, KEYS), F32),
        ),
        in_specs=[vmem] * 6,
        out_specs=(vmem,) * 4,
        scratch_shapes=scratch,
        compiler_params=pltpu.CompilerParams(
            collective_id=0, has_side_effects=True, vmem_limit_bytes=56 * 1024 * 1024),
        cost_estimate=pl.CostEstimate(flops=4_000_000_000, bytes_accessed=3_000_000, transcendentals=2_200_000),
    )(query_pair, key_pair, value_pair, pair_bias, residue_mask.reshape(1, -1), grad_output)


def solution(mesh):
    in_specs = (
        P("row", "col", None),
        P("row", "col", None),
        P("row", "col", None),
        P(None, "col", "row"),
        P("row"),
        P("row", "col", None),
    )
    out_specs = (
        P("row", "col", None),
        P("row", "col", None),
        P("row", "col", None),
        P(None, "col", "row"),
    )
    return jax.shard_map(
        on_device, mesh=mesh, in_specs=in_specs, out_specs=out_specs, check_vma=False
    )
```

time: 595 us -> 90.3 us (0.15)
  the two profiles are of different devices: /device:TPU:1 before, /device:TPU:28 now
where the time goes in v1:
time: 90.3 us; the launch traced here: 90.1 us
  Pallas kernels  84.2 us (93%)
  local copies, waits for them, and re-layouts  5.26 us (6%)
    pallas_call x1, Pallas kernels, on_device(): pl.pallas_call(kernel, out_shape=(shape((1,) + block, F32), shape((1,) +...  84.2 us
    unnamed x8, local copies, waits for them, and re-layouts  5.26 us

profile of v1, /device:TPU:28, one launch (start us, length us, event | category | flops | bytes accessed | tf_op | source)
XLA Modules:
  0.0 90.1 jit_solution(3950551505666163560)
XLA Ops:
  0.6 84.2 %shard_map.93 = (f32[1,128,128]{2,1,0:T(8,128)}, f32[1,128,128]{2,1,0:T(8,128)}, f32[1,128,128]{2,1,0:T(8,128)}, f32[4,128,512]{2,1,0:T(8,128)}) custom-call(bf16[1,128,128]{2,1,0:T(8,128)(2,1)} %q_ref.1, bf16[1,128,128]{2,1,0:T(8,128)(2,1)} %k_ref.1, bf16[1,128,128]{2,1,0:T(8,128)(2,1)} %v_ref.1, bf16[4,128,512]{2,1,0:T(8,128)(2,1)} %b_ref.1, ...), custom_call_target="tpu_custom_call" | custom-call | flops 4000000000 | bytes 3000000 | tf_op jit(solution)/shard_map/pallas_call | solution.py:388
  84.8 0.0 copy-start.1
  84.8 1.5 %copy.14 = f32[1,128,128]{2,1,0:T(8,128)} copy(f32[1,128,128]{2,1,0:T(8,128)} %get-tuple-element.8) | data formatting | bytes 131072
  86.3 0.0 copy-done.1
  86.3 0.0 copy-start
  86.3 0.6 copy.15
  87.0 0.2 copy-done
  87.2 0.6 copy.16
  87.8 2.3 %copy.17 = f32[4,128,512]{2,1,0:T(8,128)} copy(f32[4,128,512]{2,1,0:T(8,128)} %get-tuple-element.11) | data formatting | bytes 2097152
Async XLA Ops:
  84.8 1.5 %copy-start.1 = (f32[1,128,128]{2,1,0:T(8,128)S(1)}, f32[1,128,128]{2,1,0:T(8,128)}, u32[]{:S(2)}) copy-start(f32[1,128,128]{2,1,0:T(8,128)} %get-tuple-element.9) | copy-start | bytes 196612
  86.3 0.9 copy-start

commit v2 on v0

v2 whole, which is shorter than its diff:
```python
import math

import jax
import jax.numpy as jnp
from jax import lax
from jax.experimental import pallas as pl
from jax.experimental.pallas import tpu as pltpu
from jax.sharding import PartitionSpec as P

HEADS = 4
HEAD_DIM = 32
ROWS = 8
PLANES = 8
BLOCK = 128
WIDE = 512
HALF = 256
MESH = pl.DeviceIdType.MESH
LOG2E = 1.4426950408889634
SCALE = 1.0 / math.sqrt(HEAD_DIM)
F32 = jnp.float32
BF16 = jnp.bfloat16
FAR_FIRST = (4, 3, 5, 2, 6, 1, 7, 0)
CHUNKS = 4
LINES = 8
K, Q, V, G = 0, 1, 2, 3


def wait_copy(ref, sem):
    pltpu.make_async_copy(ref, ref, sem).wait()


def tn(a, b):
    return lax.dot_general(a, b, (((0,), (0,)), ((), ())), preferred_element_type=F32)


def nt(a, b):
    return lax.dot_general(a, b, (((1,), (1,)), ((), ())), preferred_element_type=F32)


def flip(block):
    return jnp.transpose(block.astype(F32))


def kernel(
    q_ref, k_ref, v_ref, b_ref, m_ref, g_ref,
    grads_ref, own_ref, rest_ref,
    pack, swap, inb, b_swap, b_full, bias_t, db_acc, p_buf, wg_buf, local, st, coef, wl, dl,
    rr_out, rr_in, zr_in, dq_acc, dq_out, dq_in, fx_out, fx_in, dby_out, dby_in, dbo_out, rest,
    swap_s, swap_r, in_s, in_r, b_s, b_r, st_s, st_r, rr_s, rr_r, zr_s, zr_r, dq_s, dq_r,
    fx_s, fx_r, db_s, db_r,
):
    r = lax.axis_index("row")
    c = lax.axis_index("col")
    z = c // 4
    yl = (c // 2) % 2
    core = c % 2
    head = core * 2 + yl
    other = (r, c + 1 - 2 * core)
    across = (r, c + 2 - 4 * yl)

    def place(row, plane, y):
        return (row, plane * 4 + y * 2 + core)

    def remote(src, dst, send, recv, target):
        return pltpu.make_async_remote_copy(
            src, dst, send, recv, device_id=target, device_id_type=MESH)

    def either(mine, local_copy, remote_copy):
        @pl.when(mine)
        def _():
            local_copy.start()

        @pl.when(jnp.logical_not(mine))
        def _():
            remote_copy.start()

    barrier = pltpu.get_barrier_semaphore()

    def greet(target):
        pl.semaphore_signal(barrier, inc=1, device_id=target, device_id_type=MESH)

    home = z == r
    for i in range(ROWS):
        for y in range(2):
            @pl.when(jnp.logical_not(jnp.logical_and(home, jnp.logical_and(i == r, y == yl))))
            def _():
                greet(place(i, r, y))
    for d in range(ROWS):
        for y in range(2):
            if d or y:
                greet(place((r + d) % ROWS, z, (yl + y) % 2))
    for d in range(1, PLANES):
        greet(place(r, (z + d) % PLANES, yl))
    greet(other)

    for kind, ref in ((K, k_ref), (Q, q_ref), (V, v_ref), (G, g_ref)):
        turned = flip(ref[0]).astype(BF16)
        keep = jnp.where(core == 0, turned[:64], turned[64:])
        give = jnp.where(core == 0, turned[64:], turned[:64])
        for y in range(2):
            pack[kind, y, core] = keep[y * HEAD_DIM:(y + 1) * HEAD_DIM]
            swap[kind, y] = give[y * HEAD_DIM:(y + 1) * HEAD_DIM]
    pl.semaphore_wait(barrier, 39 - home.astype(jnp.int32))

    def swap_copy(kind):
        return remote(swap.at[kind], pack.at[kind, :, core], swap_s.at[kind], swap_r.at[kind], other)

    def bias_core():
        return remote(b_ref.at[pl.ds(2 * (1 - core), 2)], b_swap, b_s.at[0], b_r.at[0], other)

    def bias_near():
        return remote(
            b_ref.at[2 * core + 1 - yl], b_full.at[yl, core], b_s.at[1], b_r.at[1], across)

    def bias_far():
        return remote(
            b_swap.at[1 - yl], b_full.at[yl, 1 - core], b_s.at[2], b_r.at[2], across)

    def kv_copy(kind, plane, y):
        return remote(
            pack.at[kind, y], inb.at[kind, r, yl], in_s.at[kind], in_r.at[kind, r],
            place(z, plane, y))

    def qg_copy(kind, row, y):
        return remote(
            pack.at[kind, y], inb.at[kind, r, yl], in_s.at[kind], in_r.at[kind, r],
            place(row, z, y))

    def keep_copy(kind, y):
        return pltpu.make_async_copy(pack.at[kind, y], inb.at[kind, r, yl], in_r.at[kind, r])

    def send_kv(kind):
        wait_copy(pack.at[kind, :, 1 - core], swap_r.at[kind])
        for d in FAR_FIRST:
            plane = (z + d) % PLANES
            for y in range(2):
                if d:
                    kv_copy(kind, plane, y).start()
                else:
                    either(jnp.logical_and(home, y == yl), keep_copy(kind, y), kv_copy(kind, plane, y))

    def send_qg(kind):
        wait_copy(pack.at[kind, :, 1 - core], swap_r.at[kind])
        for d in FAR_FIRST:
            row = (r + d) % ROWS
            for y in range(2):
                if d:
                    qg_copy(kind, row, y).start()
                else:
                    either(y == yl, keep_copy(kind, y), qg_copy(kind, row, y))

    def drained(kib, sem):
        wait_copy(p_buf.at[0, pl.ds(0, kib // 2)], sem)

    def kv_sent(kind):
        @pl.when(home)
        def _():
            drained(240, in_s.at[kind])

        @pl.when(jnp.logical_not(home))
        def _():
            drained(256, in_s.at[kind])

    swap_copy(K).start()
    bias_near().start()
    bias_core().start()
    for kind in (Q, V, G):
        swap_copy(kind).start()
    send_kv(K)
    wait_copy(b_swap, b_r.at[0])
    bias_far().start()
    send_qg(Q)
    send_kv(V)
    send_qg(G)

    present = m_ref[...] == 1

    def turn_bias(block, y, cc):
        masked = jnp.where(present, block.astype(F32), -1000000000.0) * LOG2E
        start = pl.multiple_of(y * HALF + cc * BLOCK, BLOCK)
        for part in range(4):
            bias_t[part * BLOCK:(part + 1) * BLOCK, pl.ds(start, BLOCK)] = jnp.transpose(
                masked[:, part * BLOCK:(part + 1) * BLOCK])

    turn_bias(b_ref[head], yl, core)
    turn_bias(b_swap[yl], yl, 1 - core)
    db_acc[...] = jnp.zeros_like(db_acc)
    dq_acc[...] = jnp.zeros_like(dq_acc)
    wait_copy(b_full.at[1 - yl, core], b_r.at[1])
    turn_bias(b_full[1 - yl, core], 1 - yl, core)
    wait_copy(b_full.at[1 - yl, 1 - core], b_r.at[2])
    turn_bias(b_full[1 - yl, 1 - core], 1 - yl, 1 - core)

    def wide(kind, i):
        return jnp.concatenate([inb[kind, i, y, cc] for y in range(2) for cc in range(2)], axis=1)

    def folded(block):
        return block.reshape(BLOCK // LINES, LINES, HALF)

    def first(t, carried):
        i = (r + t) % ROWS
        wait_copy(inb.at[K, i], in_r.at[K, i])
        wait_copy(inb.at[Q, i], in_r.at[Q, i])
        keys, queries = flip(wide(K, i)).astype(BF16), wide(Q, i)
        for part in range(2):
            cols = slice(part * HALF, (part + 1) * HALF)
            for chunk in range(CHUNKS):
                rows = slice(chunk * BLOCK, (chunk + 1) * BLOCK)
                s = jnp.dot(keys[rows], queries[:, cols], preferred_element_type=F32)
                s = folded(s * (SCALE * LOG2E) + bias_t[rows, cols])
                top = jnp.max(s, axis=0)
                p = jnp.exp2(s - top)
                p_buf[i, rows, cols] = p.reshape(BLOCK, HALF)
                local[0, i, chunk, :, cols] = top
                local[1, i, chunk, :, cols] = jnp.sum(p, axis=0)
        return carried

    lax.fori_loop(0, ROWS, first, 0)

    def st_copy(part, d):
        return remote(
            st.at[part, r], st.at[part, r], st_s.at[part], st_r.at[part],
            place((r + d) % ROWS, z, yl))

    for part in range(2):
        cols = slice(part * HALF, (part + 1) * HALF)

        def second(t, carried):
            i = (r + t) % ROWS
            if part == 0:
                wait_copy(inb.at[V, i], in_r.at[V, i])
                wait_copy(inb.at[G, i], in_r.at[G, i])
            values = flip(wide(V, i)).astype(BF16)
            gradients = jnp.concatenate([inb[G, i, part, cc] for cc in range(2)], axis=1)
            for chunk in range(CHUNKS):
                rows = slice(chunk * BLOCK, (chunk + 1) * BLOCK)
                wg = jnp.dot(values[rows], gradients, preferred_element_type=F32)
                wg_buf[i, rows, cols] = wg
                local[2, i, chunk, :, cols] = jnp.sum(folded(p_buf[i, rows, cols] * wg), axis=0)
            return carried

        lax.fori_loop(0, ROWS, second, 0)
        tops = local[0, :, :, :, cols].reshape(ROWS, CHUNKS * LINES, HALF)
        top = jnp.max(tops, axis=1, keepdims=True)
        scale = jnp.exp2(tops - top)
        total = jnp.sum(scale * local[1, :, :, :, cols].reshape(tops.shape), axis=1)
        dot = jnp.sum(scale * local[2, :, :, :, cols].reshape(tops.shape), axis=1)
        top = top.reshape(ROWS, HALF)
        st[part, r, 0] = top + jnp.log(total) * LOG2E
        st[part, r, 1] = dot / total
        for d in FAR_FIRST[:-1]:
            st_copy(part, d).start()

    for part in range(2):
        cols = slice(part * HALF, (part + 1) * HALF)
        wait_copy(st.at[part, pl.ds(0, ROWS - 1)], st_r.at[part])
        peak = st[part, 0, 0]
        for d in range(1, ROWS):
            peak = jnp.maximum(peak, st[part, d, 0])
        norm = jnp.zeros_like(peak)
        delta = jnp.zeros_like(peak)
        for d in range(ROWS):
            part_of = jnp.exp2(st[part, d, 0] - peak)
            norm += part_of
            delta += part_of * st[part, d, 1]
        inverse = 1.0 / norm
        delta = delta * inverse
        for i in range(ROWS):
            for chunk in range(CHUNKS):
                coef[i, chunk, :, cols] = jnp.exp2(local[0, i, chunk, :, cols] - peak[i:i + 1]) * inverse[i:i + 1]
            coef[i, CHUNKS, :, cols] = jnp.broadcast_to(delta[i:i + 1], (LINES, HALF))

    def rr_copy(s, t, half):
        return remote(
            rr_out.at[s * 8 + t], rr_in.at[r, yl], rr_s, rr_r.at[r * 2 + yl],
            place((r + 1 + t) % ROWS, z, half))

    def zr_copy(row, hl):
        return remote(
            rr_in.at[row, hl], zr_in.at[z, hl], zr_s, zr_r.at[z],
            place(r, row, yl))

    def dq_copy(t, y):
        return remote(
            dq_out.at[t * 2 + y], dq_in.at[r, yl], dq_s, dq_r,
            place((r + 1 + t) % ROWS, z, y))

    def third(s):
        half = (yl + s) % 2
        rows = pl.ds(pl.multiple_of(half * HALF, HALF), HALF)

        def step(t, carried):
            i = (r + 1 + t) % ROWS
            for part in range(2):
                cols = slice(part * HALF, (part + 1) * HALF)
                delta = coef[i, CHUNKS, :, cols]
                for sub in range(2):
                    rows = pl.ds(pl.multiple_of(half * HALF + sub * BLOCK, BLOCK), BLOCK)
                    out = slice(sub * BLOCK, (sub + 1) * BLOCK)
                    w = folded(p_buf[i, rows, cols]) * coef[i, half * 2 + sub, :, cols]
                    ds = (w * (folded(wg_buf[i, rows, cols]) - delta)).reshape(BLOCK, HALF)
                    w = w.reshape(BLOCK, HALF)
                    db_acc[rows, cols] += ds
                    wl[out, cols] = w.astype(BF16)
                    dl[out, cols] = ds.astype(BF16)
            rr_out[s * 8 + t, 0] = nt(wide(Q, i), dl[...]).astype(BF16)
            rr_out[s * 8 + t, 1] = nt(wide(G, i), wl[...]).astype(BF16)
            mine = jnp.logical_and(t == ROWS - 1, half == yl)
            either(
                mine,
                pltpu.make_async_copy(rr_out.at[s * 8 + t], rr_in.at[r, yl], rr_r.at[r * 2 + yl]),
                rr_copy(s, t, half))
            keys = jnp.concatenate([inb[K, i, half, cc] for cc in range(2)], axis=1)
            total = dq_acc[i] + jnp.dot(keys, dl[...], preferred_element_type=F32)
            if s == 0:
                dq_acc[i] = total
            else:
                for y in range(2):
                    dq_out[t * 2 + y] = total[:, y * HALF:(y + 1) * HALF].astype(BF16)
                    either(
                        jnp.logical_and(t == ROWS - 1, y == yl),
                        pltpu.make_async_copy(dq_out.at[t * 2 + y], dq_in.at[r, yl], dq_r),
                        dq_copy(t, y))
            return carried

        lax.fori_loop(0, ROWS, step, 0)
        away = pl.ds(pl.multiple_of((1 - yl) * HALF, HALF), HALF)
        turned = flip(db_acc[rows, away]).astype(BF16)
        for cc in range(2):
            dby_out[s, cc] = turned[cc * BLOCK:(cc + 1) * BLOCK]
        dby_copy(s, half).start()

    def dby_copy(s, half):
        return remote(dby_out.at[s], dby_in.at[half], db_s.at[s], db_r.at[half], across)

    third(0)
    third(1)

    def forward(u, carried):
        s, t = u // 8, u % 8
        row = (r + 2 * ROWS - 1 - t) % ROWS
        hl = (yl + s) % 2
        wait_copy(rr_in.at[row, hl], rr_r.at[row * 2 + hl])

        @pl.when(row != z)
        def _():
            zr_copy(row, hl).start()
        return carried

    lax.fori_loop(0, 16, forward, 0)

    near = pl.ds(pl.multiple_of(yl * HALF + core * BLOCK, BLOCK), BLOCK)
    far = pl.ds(pl.multiple_of(yl * HALF + (1 - core) * BLOCK, BLOCK), BLOCK)
    turned = flip(db_acc[:, far]).astype(BF16)
    for half in range(2):
        dbo_out[half] = turned[:, half * HALF:(half + 1) * HALF]
    twin = core * 2 + 1 - yl

    def dbo_copy():
        return remote(dbo_out, rest.at[head], db_s.at[2], db_r.at[2], other)

    def dbt_copy(half):
        return remote(
            dby_in.at[half, 1 - core], rest.at[twin, half], db_s.at[3 + half], db_r.at[3 + half], other)

    dbo_copy().start()
    own_ref[...] = flip(db_acc[:, near])
    for s in range(2):
        half = (yl + 1 + s) % 2
        wait_copy(dby_in.at[half], db_r.at[half])
        dbt_copy(half).start()

    total = jnp.zeros((2, HEAD_DIM, HALF), F32)
    wait_copy(dq_in, dq_r)
    for row in range(ROWS):
        total += dq_in[row].astype(F32)

    def hand_over(slot, total):
        low, high = total[:, :, :BLOCK], total[:, :, BLOCK:]
        mine = jnp.where(core == 0, low, high)
        fx_out[slot] = jnp.where(core == 0, high, low)
        grads_ref[slot, core] = mine

    def fx_copy(start, size):
        part = pl.ds(start, size)
        return remote(fx_out.at[part], fx_in.at[part], fx_s.at[start], fx_r.at[start], other)

    hand_over(0, total)
    fx_copy(0, 1).start()

    rest_ref[twin] = dby_in[:, core]
    wait_copy(rest.at[2 * (1 - core) + yl], db_r.at[2])
    for half in range(2):
        wait_copy(rest.at[2 * (1 - core) + 1 - yl, half], db_r.at[3 + half])
    for y in range(2):
        rest_ref[2 * (1 - core) + y] = rest[2 * (1 - core) + y]
    rest_ref[head] = jnp.zeros((2, BLOCK, HALF), BF16)
    wait_copy(fx_in.at[pl.ds(0, 1)], fx_r.at[0])
    grads_ref[0, 1 - core] = fx_in[0]

    total = rr_in[z].astype(F32)
    for d in (1, 7, 2, 6, 3, 5, 4):
        plane = (z + d) % PLANES
        wait_copy(zr_in.at[plane], zr_r.at[plane])
        total += zr_in[plane].astype(F32)
    hand_over(1, total[:, 0])
    hand_over(2, total[:, 1])
    fx_copy(1, 2).start()

    for kind in (K, Q, V, G):
        swap_copy(kind).wait_send()
        if kind in (Q, G):
            drained(240, in_s.at[kind])
        else:
            kv_sent(kind)
    bias_core().wait_send()
    bias_near().wait_send()
    bias_far().wait_send()
    for part in range(2):
        wait_copy(st.at[part, pl.ds(0, ROWS - 1)], st_s.at[part])
    drained(480, rr_s)
    drained(448, zr_s)
    drained(240, dq_s)
    for s in range(2):
        dby_copy(s, (yl + s) % 2).wait_send()
        dbt_copy(s).wait_send()
    dbo_copy().wait_send()
    fx_copy(0, 1).wait_send()
    fx_copy(1, 2).wait_send()
    wait_copy(fx_in.at[pl.ds(1, 2)], fx_r.at[1])
    for slot in (1, 2):
        grads_ref[slot, 1 - core] = fx_in[slot]


def finish(grads_ref, own_ref, rest_ref, dq_ref, dk_ref, dv_ref, db_ref):
    c = lax.axis_index("col")
    head = (c % 2) * 2 + (c // 2) % 2
    for slot, ref, scale in ((0, dq_ref, SCALE), (1, dk_ref, SCALE), (2, dv_ref, None)):
        turned = jnp.transpose(grads_ref[slot].reshape(BLOCK, BLOCK))
        ref[0] = turned if scale is None else turned * scale
    for h in range(HEADS):
        for half in range(2):
            db_ref[h, :, half * HALF:(half + 1) * HALF] = rest_ref[h, half].astype(F32)
    db_ref[head] = own_ref[...]


def on_device(query_pair, key_pair, value_pair, pair_bias, residue_mask, grad_output):
    dma = pltpu.SemaphoreType.DMA
    vm = pltpu.VMEM
    scratch = [
        vm((4, 2, 2, HEAD_DIM, BLOCK), BF16),
        vm((4, 2, HEAD_DIM, BLOCK), BF16),
        vm((4, ROWS, 2, 2, HEAD_DIM, BLOCK), BF16),
        vm((2, BLOCK, WIDE), BF16),
        vm((2, 2, BLOCK, WIDE), BF16),
        vm((WIDE, WIDE), F32),
        vm((WIDE, WIDE), F32),
        vm((ROWS, WIDE, WIDE), F32),
        vm((ROWS, WIDE, WIDE), F32),
        vm((3, ROWS, CHUNKS, LINES, WIDE), F32),
        vm((2, ROWS, 2, ROWS, HALF), F32),
        vm((ROWS, CHUNKS + 1, LINES, WIDE), F32),
        vm((HALF, WIDE), BF16),
        vm((HALF, WIDE), BF16),
        vm((2 * ROWS, 2, HEAD_DIM, HALF), BF16),
        vm((ROWS, 2, 2, HEAD_DIM, HALF), BF16),
        vm((PLANES, 2, 2, HEAD_DIM, HALF), BF16),
        vm((ROWS, HEAD_DIM, WIDE), F32),
        vm((2 * ROWS, HEAD_DIM, HALF), BF16),
        vm((ROWS, 2, HEAD_DIM, HALF), BF16),
        vm((3, 2, HEAD_DIM, BLOCK), F32),
        vm((3, 2, HEAD_DIM, BLOCK), F32),
        vm((2, 2, BLOCK, HALF), BF16),
        vm((2, 2, BLOCK, HALF), BF16),
        vm((2, BLOCK, HALF), BF16),
        vm((HEADS, 2, BLOCK, HALF), BF16),
        dma((4,)), dma((4,)), dma((4,)), dma((4, 8)), dma((3,)), dma((3,)),
        dma((2,)), dma((2,)), dma, dma((16,)), dma, dma((8,)),
        dma, dma, dma((2,)), dma((2,)), dma((5,)), dma((5,)),
    ]
    vmem = pl.BlockSpec(memory_space=pltpu.VMEM)
    shape = jax.ShapeDtypeStruct
    parts = pl.pallas_call(
        kernel,
        out_shape=(
            shape((3, 2, 2, HEAD_DIM, BLOCK), F32),
            shape((BLOCK, WIDE), F32),
            shape((HEADS, 2, BLOCK, HALF), BF16),
        ),
        in_specs=[vmem] * 6,
        out_specs=(vmem,) * 3,
        scratch_shapes=scratch,
        compiler_params=pltpu.CompilerParams(
            collective_id=0, has_side_effects=True, vmem_limit_bytes=56 * 1024 * 1024),
        cost_estimate=pl.CostEstimate(flops=4_000_000_000, bytes_accessed=3_000_000, transcendentals=2_200_000),
    )(query_pair, key_pair, value_pair, pair_bias, residue_mask.reshape(1, -1), grad_output)
    pair = shape((1, BLOCK, BLOCK), F32)
    return pl.pallas_call(
        finish,
        out_shape=(pair, pair, pair, shape((HEADS, BLOCK, WIDE), F32)),
        in_specs=[vmem] * 3,
        out_specs=(vmem,) * 4,
        compiler_params=pltpu.CompilerParams(vmem_limit_bytes=60 * 1024 * 1024),
        cost_estimate=pl.CostEstimate(flops=1_000_000, bytes_accessed=2_500_000, transcendentals=0),
    )(*parts)


def solution(mesh):
    in_specs = (
        P("row", "col", None),
        P("row", "col", None),
        P("row", "col", None),
        P(None, "col", "row"),
        P("row"),
        P("row", "col", None),
    )
    out_specs = (
        P("row", "col", None),
        P("row", "col", None),
        P("row", "col", None),
        P(None, "col", "row"),
    )
    return jax.shard_map(
        on_device, mesh=mesh, in_specs=in_specs, out_specs=out_specs, check_vma=False
    )
```

time: 595 us -> 70.3 us (0.12)
  waiting for transfers between devices: 426 us -> 0 us
  Pallas kernels: 0 us -> 69.6 us
  matrix products: 59.9 us -> 0 us
  local copies, waits for them, and re-layouts: 48.3 us -> 0 us
  blocking collectives: 26.5 us -> 0 us
  between operations: 13.9 us -> 0.64 us
  starting transfers between devices: 11.1 us -> 0 us
  other arithmetic: 6.32 us -> 0 us
    ppermute x64 -> x0, waiting for transfers between devices: 190 us -> none  [shifted(): return lax.ppermute(value, axis, pairs)]
    reduce_scatter x1 -> x0, waiting for transfers between devices: 121 us -> none  [on_device(): lax.psum_scatter(bias_acc, 'row', scatter_dimension=2, tiled=True)]
    all_gather x2 -> x0, waiting for transfers between devices: 115 us -> none  [the longest x1 75.9 us: on_device(): lax.all_gather(pair_bias, 'row', axis=2, tiled=True)]
    pallas_call x0 -> x2, Pallas kernels: none -> 69.6 us  [the longest x1 67.2 us: on_device(): pl.pallas_call(kernel, out_shape=(shape((3, 2, 2, HEAD_DIM, BLOCK), F32),...]
    dot_general x162 -> x0, matrix products: 59.9 us -> none  [the longest x32 31.2 us: backward_block(): jnp.einsum('rjhd,rkhd->hrjk', grad_heads, value_heads, preferred_element_...]
    dynamic_slice x64 -> x0, local copies, waits for them, and re-layouts: 33.7 us -> none  [scores_of(): lax.dynamic_slice_in_dim(masked_bias, offset, length, 2).astype(jnp.float32)]
    all_gather x1 -> x0, blocking collectives: 26.5 us -> none  [on_device(): lax.all_gather(residue_mask.astype(jnp.bfloat16), 'row', axis=0, tiled=True)]
    ppermute x64 -> x0, starting transfers between devices: 10.9 us -> none  [shifted(): return lax.ppermute(value, axis, pairs)]
  transfers between devices with their start and end apart: 67 -> 0, of which waited for: 65 -> 0; matrix products, arithmetic and copies ran while one was open for 16% -> 0% of each run, Pallas kernels for 0% -> 0%
where the time goes in v2:
time: 70.3 us; the launch traced here: 70.2 us
  Pallas kernels  69.6 us (99%)
    pallas_call x1, Pallas kernels, on_device(): pl.pallas_call(kernel, out_shape=(shape((3, 2, 2, HEAD_DIM, BLOCK), F32),...  67.2 us
    pallas_call x1, Pallas kernels, on_device(): pl.pallas_call(finish, out_shape=(pair, pair, pair, shape((HEADS, BLOCK,...  2.36 us

profile of v2, /device:TPU:1, one launch (start us, length us, event | category | flops | bytes accessed | tf_op | source)
XLA Modules:
  0.0 70.2 jit_solution(10426763547941033694)
XLA Ops:
  0.6 67.2 %shard_map.93 = (f32[3,2,2,32,128]{4,3,2,1,0:T(8,128)}, f32[128,512]{1,0:T(8,128)}, bf16[4,2,128,256]{3,2,1,0:T(8,128)(2,1)}) custom-call(bf16[1,128,128]{2,1,0:T(8,128)(2,1)} %q_ref.1, bf16[1,128,128]{2,1,0:T(8,128)(2,1)} %k_ref.1, bf16[1,128,128]{2,1,0:T(8,128)(2,1)} %v_ref.1, bf16[4,128,512]{2,1,0:T(8,128)(2,1)} %b_ref.1, s32[1,512]{1,0:T(1,128)} %bitcast.1, ...), custom_call_target="tpu_custom_call" | custom-call | flops 4000000000 | bytes 3000000 | tf_op jit(solution)/shard_map/pallas_call | solution.py:483
  67.8 2.4 %shard_map.94 = (f32[1,128,128]{2,1,0:T(8,128)}, f32[1,128,128]{2,1,0:T(8,128)}, f32[1,128,128]{2,1,0:T(8,128)}, f32[4,128,512]{2,1,0:T(8,128)}) custom-call(f32[3,2,2,32,128]{4,3,2,1,0:T(8,128)} %get-tuple-element.7.grads_ref, f32[128,512]{1,0:T(8,128)} %get-tuple-element.8.own_ref, bf16[4,2,128,256]{3,2,1,0:T(8,128)(2,1)} %get-tuple-element.9.rest_ref), custom_call_target="tpu_custom_call" | custom-call | flops 1000000 | bytes 2500000 | tf_op jit(solution)/shard_map/pallas_call | solution.py:498

commit v3 on v2

--- a/solution.py
+++ b/solution.py
@@ -44,9 +44,9 @@
 def kernel(
     q_ref, k_ref, v_ref, b_ref, m_ref, g_ref,
     grads_ref, own_ref, rest_ref,
-    pack, swap, inb, b_swap, b_full, bias_t, db_acc, p_buf, wg_buf, local, st, coef, wl, dl,
+    pack, swap, inb, flipped, b_swap, b_full, bias_t, db_acc, p_buf, wg_buf, local, st, coef, wl, dl,
     rr_out, rr_in, zr_in, dq_acc, dq_out, dq_in, fx_out, fx_in, dby_out, dby_in, dbo_out, rest,
-    swap_s, swap_r, in_s, in_r, b_s, b_r, st_s, st_r, rr_s, rr_r, zr_s, zr_r, dq_s, dq_r,
+    swap_s, swap_r, in_s, in_r, tree_s, b_s, b_r, st_s, st_r, rr_s, rr_r, zr_s, zr_r, dq_s, dq_r,
     fx_s, fx_r, db_s, db_r,
 ):
     r = lax.axis_index("row")
@@ -126,6 +126,19 @@
             pack.at[kind, y], inb.at[kind, r, yl], in_s.at[kind], in_r.at[kind, r],
             place(row, z, y))
 
+    def tree_copy(kind, hi, d):
+        i = hi * 4 + r % 4
+        return remote(
+            inb.at[kind, i], inb.at[kind, i], tree_s.at[kind], in_r.at[kind, i],
+            place((r // 4) * 4 + (r + d) % 4, z, yl))
+
+    def tree_qg(kind):
+        for step in range(2):
+            hi = (r // 4 + step) % 2
+            wait_copy(inb.at[kind, hi * 4 + r % 4], in_r.at[kind, hi * 4 + r % 4])
+            for d in (2, 1, 3):
+                tree_copy(kind, hi, d).start()
+
     def keep_copy(kind, y):
         return pltpu.make_async_copy(pack.at[kind, y], inb.at[kind, r, yl], in_r.at[kind, r])
 
@@ -141,7 +154,7 @@
 
     def send_qg(kind):
         wait_copy(pack.at[kind, :, 1 - core], swap_r.at[kind])
-        for d in FAR_FIRST:
+        for d in (4, 0):
             row = (r + d) % ROWS
             for y in range(2):
                 if d:
@@ -166,12 +179,14 @@
     bias_core().start()
     for kind in (Q, V, G):
         swap_copy(kind).start()
+    send_qg(Q)
     send_kv(K)
+    send_qg(G)
     wait_copy(b_swap, b_r.at[0])
     bias_far().start()
-    send_qg(Q)
     send_kv(V)
-    send_qg(G)
+    tree_qg(Q)
+    tree_qg(G)
 
     present = m_ref[...] == 1
 
@@ -200,7 +215,10 @@
     def first(t, carried):
         i = (r + t) % ROWS
         wait_copy(inb.at[K, i], in_r.at[K, i])
-        wait_copy(inb.at[Q, i], in_r.at[Q, i])
+
+        @pl.when(i % 4 != r % 4)
+        def _():
+            wait_copy(inb.at[Q, i], in_r.at[Q, i])
         keys, queries = flip(wide(K, i)).astype(BF16), wide(Q, i)
         for part in range(2):
             cols = slice(part * HALF, (part + 1) * HALF)
@@ -229,8 +247,14 @@
             i = (r + t) % ROWS
             if part == 0:
                 wait_copy(inb.at[V, i], in_r.at[V, i])
-                wait_copy(inb.at[G, i], in_r.at[G, i])
-            values = flip(wide(V, i)).astype(BF16)
+
+                @pl.when(i % 4 != r % 4)
+                def _():
+                    wait_copy(inb.at[G, i], in_r.at[G, i])
+                values = flip(wide(V, i)).astype(BF16)
+                flipped[i] = values
+            else:
+                values = flipped[i]
             gradients = jnp.concatenate([inb[G, i, part, cc] for cc in range(2)], axis=1)
             for chunk in range(CHUNKS):
                 rows = slice(chunk * BLOCK, (chunk + 1) * BLOCK)
@@ -273,7 +297,7 @@
     def rr_copy(s, t, half):
         return remote(
             rr_out.at[s * 8 + t], rr_in.at[r, yl], rr_s, rr_r.at[r * 2 + yl],
-            place((r + 1 + t) % ROWS, z, half))
+            place((r + z + 1 + t) % ROWS, z, half))
 
     def zr_copy(row, hl):
         return remote(
@@ -283,14 +307,14 @@
     def dq_copy(t, y):
         return remote(
             dq_out.at[t * 2 + y], dq_in.at[r, yl], dq_s, dq_r,
-            place((r + 1 + t) % ROWS, z, y))
+            place((r + z + 1 + t) % ROWS, z, y))
 
     def third(s):
         half = (yl + s) % 2
         rows = pl.ds(pl.multiple_of(half * HALF, HALF), HALF)
 
         def step(t, carried):
-            i = (r + 1 + t) % ROWS
+            i = (r + z + 1 + t) % ROWS
             for part in range(2):
                 cols = slice(part * HALF, (part + 1) * HALF)
                 delta = coef[i, CHUNKS, :, cols]
@@ -305,7 +329,7 @@
                     dl[out, cols] = ds.astype(BF16)
             rr_out[s * 8 + t, 0] = nt(wide(Q, i), dl[...]).astype(BF16)
             rr_out[s * 8 + t, 1] = nt(wide(G, i), wl[...]).astype(BF16)
-            mine = jnp.logical_and(t == ROWS - 1, half == yl)
+            mine = jnp.logical_and(i == r, half == yl)
             either(
                 mine,
                 pltpu.make_async_copy(rr_out.at[s * 8 + t], rr_in.at[r, yl], rr_r.at[r * 2 + yl]),
@@ -318,7 +342,7 @@
                 for y in range(2):
                     dq_out[t * 2 + y] = total[:, y * HALF:(y + 1) * HALF].astype(BF16)
                     either(
-                        jnp.logical_and(t == ROWS - 1, y == yl),
+                        jnp.logical_and(i == r, y == yl),
                         pltpu.make_async_copy(dq_out.at[t * 2 + y], dq_in.at[r, yl], dq_r),
                         dq_copy(t, y))
             return carried
@@ -338,7 +362,7 @@
 
     def forward(u, carried):
         s, t = u // 8, u % 8
-        row = (r + 2 * ROWS - 1 - t) % ROWS
+        row = (r + 2 * ROWS - z - 1 - t) % ROWS
         hl = (yl + s) % 2
         wait_copy(rr_in.at[row, hl], rr_r.at[row * 2 + hl])
 
@@ -410,7 +434,8 @@
     for kind in (K, Q, V, G):
         swap_copy(kind).wait_send()
         if kind in (Q, G):
-            drained(240, in_s.at[kind])
+            drained(48, in_s.at[kind])
+            drained(192, tree_s.at[kind])
         else:
             kv_sent(kind)
     bias_core().wait_send()
@@ -451,6 +476,7 @@
         vm((4, 2, 2, HEAD_DIM, BLOCK), BF16),
         vm((4, 2, HEAD_DIM, BLOCK), BF16),
         vm((4, ROWS, 2, 2, HEAD_DIM, BLOCK), BF16),
+        vm((ROWS, WIDE, HEAD_DIM), BF16),
         vm((2, BLOCK, WIDE), BF16),
         vm((2, 2, BLOCK, WIDE), BF16),
         vm((WIDE, WIDE), F32),
@@ -474,7 +500,7 @@
         vm((2, 2, BLOCK, HALF), BF16),
         vm((2, BLOCK, HALF), BF16),
         vm((HEADS, 2, BLOCK, HALF), BF16),
-        dma((4,)), dma((4,)), dma((4,)), dma((4, 8)), dma((3,)), dma((3,)),
+        dma((4,)), dma((4,)), dma((4,)), dma((4, 8)), dma((4,)), dma((3,)), dma((3,)),
         dma((2,)), dma((2,)), dma, dma((16,)), dma, dma((8,)),
         dma, dma, dma((2,)), dma((2,)), dma((5,)), dma((5,)),
     ]

time: 70.3 us -> 67.6 us (0.962)
  Pallas kernels: 69.6 us -> 66.8 us
    pallas_call x1, Pallas kernels: 67.2 us -> 64.5 us  [on_device(): pl.pallas_call(kernel, out_shape=(shape((3, 2, 2, HEAD_DIM, BLOCK), F32),...]
where the time goes in v3:
time: 67.6 us; the launch traced here: 67.5 us
  Pallas kernels  66.8 us (99%)
    pallas_call x1, Pallas kernels, on_device(): pl.pallas_call(kernel, out_shape=(shape((3, 2, 2, HEAD_DIM, BLOCK), F32),...  64.5 us
    pallas_call x1, Pallas kernels, on_device(): pl.pallas_call(finish, out_shape=(pair, pair, pair, shape((HEADS, BLOCK,...  2.36 us

profile of v3, /device:TPU:1, one launch (start us, length us, event | category | flops | bytes accessed | tf_op | source)
XLA Modules:
  0.0 67.5 jit_solution(16984461814136845904)
XLA Ops:
  0.6 64.5 %shard_map.93 = (f32[3,2,2,32,128]{4,3,2,1,0:T(8,128)}, f32[128,512]{1,0:T(8,128)}, bf16[4,2,128,256]{3,2,1,0:T(8,128)(2,1)}) custom-call(bf16[1,128,128]{2,1,0:T(8,128)(2,1)} %q_ref.1, bf16[1,128,128]{2,1,0:T(8,128)(2,1)} %k_ref.1, bf16[1,128,128]{2,1,0:T(8,128)(2,1)} %v_ref.1, bf16[4,128,512]{2,1,0:T(8,128)(2,1)} %b_ref.1, s32[1,512]{1,0:T(1,128)} %bitcast.1, ...), custom_call_target="tpu_custom_call" | custom-call | flops 4000000000 | bytes 3000000 | tf_op jit(solution)/shard_map/pallas_call | solution.py:509
  65.1 2.4 %shard_map.94 = (f32[1,128,128]{2,1,0:T(8,128)}, f32[1,128,128]{2,1,0:T(8,128)}, f32[1,128,128]{2,1,0:T(8,128)}, f32[4,128,512]{2,1,0:T(8,128)}) custom-call(f32[3,2,2,32,128]{4,3,2,1,0:T(8,128)} %get-tuple-element.7.grads_ref, f32[128,512]{1,0:T(8,128)} %get-tuple-element.8.own_ref, bf16[4,2,128,256]{3,2,1,0:T(8,128)(2,1)} %get-tuple-element.9.rest_ref), custom_call_target="tpu_custom_call" | custom-call | flops 1000000 | bytes 2500000 | tf_op jit(solution)/shard_map/pallas_call | solution.py:524

commit v4 on v3

--- a/solution.py
+++ b/solution.py
@@ -212,13 +212,22 @@
     def folded(block):
         return block.reshape(BLOCK // LINES, LINES, HALF)
 
-    def first(t, carried):
-        i = (r + t) % ROWS
-        wait_copy(inb.at[K, i], in_r.at[K, i])
+    def arrive(kv, qg, i):
+        wait_copy(inb.at[kv, i], in_r.at[kv, i])
 
         @pl.when(i % 4 != r % 4)
         def _():
-            wait_copy(inb.at[Q, i], in_r.at[Q, i])
+            wait_copy(inb.at[qg, i], in_r.at[qg, i])
+
+    def first(t, carried):
+        pair = [(r + 2 * t + step) % ROWS for step in range(2)]
+        for i in pair:
+            arrive(K, Q, i)
+        for i in pair:
+            score_row(i)
+        return carried
+
+    def score_row(i):
         keys, queries = flip(wide(K, i)).astype(BF16), wide(Q, i)
         for part in range(2):
             cols = slice(part * HALF, (part + 1) * HALF)
@@ -231,9 +240,8 @@
                 p_buf[i, rows, cols] = p.reshape(BLOCK, HALF)
                 local[0, i, chunk, :, cols] = top
                 local[1, i, chunk, :, cols] = jnp.sum(p, axis=0)
-        return carried
-
-    lax.fori_loop(0, ROWS, first, 0)
+
+    lax.fori_loop(0, ROWS // 2, first, 0)
 
     def st_copy(part, d):
         return remote(
@@ -244,13 +252,16 @@
         cols = slice(part * HALF, (part + 1) * HALF)
 
         def second(t, carried):
-            i = (r + t) % ROWS
+            pair = [(r + 2 * t + step) % ROWS for step in range(2)]
             if part == 0:
-                wait_copy(inb.at[V, i], in_r.at[V, i])
-
-                @pl.when(i % 4 != r % 4)
-                def _():
-                    wait_copy(inb.at[G, i], in_r.at[G, i])
+                for i in pair:
+                    arrive(V, G, i)
+            for i in pair:
+                weight_row(i)
+            return carried
+
+        def weight_row(i):
+            if part == 0:
                 values = flip(wide(V, i)).astype(BF16)
                 flipped[i] = values
             else:
@@ -261,9 +272,8 @@
                 wg = jnp.dot(values[rows], gradients, preferred_element_type=F32)
                 wg_buf[i, rows, cols] = wg
                 local[2, i, chunk, :, cols] = jnp.sum(folded(p_buf[i, rows, cols] * wg), axis=0)
-            return carried
-
-        lax.fori_loop(0, ROWS, second, 0)
+
+        lax.fori_loop(0, ROWS // 2, second, 0)
         tops = local[0, :, :, :, cols].reshape(ROWS, CHUNKS * LINES, HALF)
         top = jnp.max(tops, axis=1, keepdims=True)
         scale = jnp.exp2(tops - top)
@@ -313,7 +323,7 @@
         half = (yl + s) % 2
         rows = pl.ds(pl.multiple_of(half * HALF, HALF), HALF)
 
-        def step(t, carried):
+        def weights(t, slot):
             i = (r + z + 1 + t) % ROWS
             for part in range(2):
                 cols = slice(part * HALF, (part + 1) * HALF)
@@ -325,29 +335,44 @@
                     ds = (w * (folded(wg_buf[i, rows, cols]) - delta)).reshape(BLOCK, HALF)
                     w = w.reshape(BLOCK, HALF)
                     db_acc[rows, cols] += ds
-                    wl[out, cols] = w.astype(BF16)
-                    dl[out, cols] = ds.astype(BF16)
-            rr_out[s * 8 + t, 0] = nt(wide(Q, i), dl[...]).astype(BF16)
-            rr_out[s * 8 + t, 1] = nt(wide(G, i), wl[...]).astype(BF16)
-            mine = jnp.logical_and(i == r, half == yl)
-            either(
-                mine,
-                pltpu.make_async_copy(rr_out.at[s * 8 + t], rr_in.at[r, yl], rr_r.at[r * 2 + yl]),
-                rr_copy(s, t, half))
+                    wl[slot, out, cols] = w.astype(BF16)
+                    dl[slot, out, cols] = ds.astype(BF16)
+
+        def products(t, slot):
+            i = (r + z + 1 + t) % ROWS
+            rr_out[s * 8 + t, 0] = nt(wide(Q, i), dl[slot]).astype(BF16)
+            rr_out[s * 8 + t, 1] = nt(wide(G, i), wl[slot]).astype(BF16)
             keys = jnp.concatenate([inb[K, i, half, cc] for cc in range(2)], axis=1)
-            total = dq_acc[i] + jnp.dot(keys, dl[...], preferred_element_type=F32)
+            total = dq_acc[i] + jnp.dot(keys, dl[slot], preferred_element_type=F32)
             if s == 0:
                 dq_acc[i] = total
             else:
                 for y in range(2):
                     dq_out[t * 2 + y] = total[:, y * HALF:(y + 1) * HALF].astype(BF16)
+
+        def send_back(t):
+            i = (r + z + 1 + t) % ROWS
+            either(
+                jnp.logical_and(i == r, half == yl),
+                pltpu.make_async_copy(rr_out.at[s * 8 + t], rr_in.at[r, yl], rr_r.at[r * 2 + yl]),
+                rr_copy(s, t, half))
+            if s:
+                for y in range(2):
                     either(
                         jnp.logical_and(i == r, y == yl),
                         pltpu.make_async_copy(dq_out.at[t * 2 + y], dq_in.at[r, yl], dq_r),
                         dq_copy(t, y))
+
+        def step(t, carried):
+            weights(2 * t, 0)
+            products(2 * t, 0)
+            weights(2 * t + 1, 1)
+            products(2 * t + 1, 1)
+            send_back(2 * t)
+            send_back(2 * t + 1)
             return carried
 
-        lax.fori_loop(0, ROWS, step, 0)
+        lax.fori_loop(0, ROWS // 2, step, 0)
         away = pl.ds(pl.multiple_of((1 - yl) * HALF, HALF), HALF)
         turned = flip(db_acc[rows, away]).astype(BF16)
         for cc in range(2):
@@ -486,8 +511,8 @@
         vm((3, ROWS, CHUNKS, LINES, WIDE), F32),
         vm((2, ROWS, 2, ROWS, HALF), F32),
         vm((ROWS, CHUNKS + 1, LINES, WIDE), F32),
-        vm((HALF, WIDE), BF16),
-        vm((HALF, WIDE), BF16),
+        vm((2, HALF, WIDE), BF16),
+        vm((2, HALF, WIDE), BF16),
         vm((2 * ROWS, 2, HEAD_DIM, HALF), BF16),
         vm((ROWS, 2, 2, HEAD_DIM, HALF), BF16),
         vm((PLANES, 2, 2, HEAD_DIM, HALF), BF16),

time: 67.6 us -> 65 us (0.962); the launches traced: 67.5 us -> 64.1 us
  Pallas kernels: 66.8 us -> 63.4 us
    pallas_call x1, Pallas kernels: 64.5 us -> 61.1 us  [on_device(): pl.pallas_call(kernel, out_shape=(shape((3, 2, 2, HEAD_DIM, BLOCK), F32),...]
where the time goes in v4:
time: 65 us; the launch traced here: 64.1 us
  Pallas kernels  63.4 us (98%)
    pallas_call x1, Pallas kernels, on_device(): pl.pallas_call(kernel, out_shape=(shape((3, 2, 2, HEAD_DIM, BLOCK), F32),...  61.1 us
    pallas_call x1, Pallas kernels, on_device(): pl.pallas_call(finish, out_shape=(pair, pair, pair, shape((HEADS, BLOCK,...  2.36 us

profile of v4, /device:TPU:1, one launch (start us, length us, event | category | flops | bytes accessed | tf_op | source)
XLA Modules:
  0.0 64.1 jit_solution(7924852858550303134)
XLA Ops:
  0.6 61.1 %shard_map.93 = (f32[3,2,2,32,128]{4,3,2,1,0:T(8,128)}, f32[128,512]{1,0:T(8,128)}, bf16[4,2,128,256]{3,2,1,0:T(8,128)(2,1)}) custom-call(bf16[1,128,128]{2,1,0:T(8,128)(2,1)} %q_ref.1, bf16[1,128,128]{2,1,0:T(8,128)(2,1)} %k_ref.1, bf16[1,128,128]{2,1,0:T(8,128)(2,1)} %v_ref.1, bf16[4,128,512]{2,1,0:T(8,128)(2,1)} %b_ref.1, s32[1,512]{1,0:T(1,128)} %bitcast.1, ...), custom_call_target="tpu_custom_call" | custom-call | flops 4000000000 | bytes 3000000 | tf_op jit(solution)/shard_map/pallas_call | solution.py:534
  61.7 2.4 %shard_map.94 = (f32[1,128,128]{2,1,0:T(8,128)}, f32[1,128,128]{2,1,0:T(8,128)}, f32[1,128,128]{2,1,0:T(8,128)}, f32[4,128,512]{2,1,0:T(8,128)}) custom-call(f32[3,2,2,32,128]{4,3,2,1,0:T(8,128)} %get-tuple-element.7.grads_ref, f32[128,512]{1,0:T(8,128)} %get-tuple-element.8.own_ref, bf16[4,2,128,256]{3,2,1,0:T(8,128)(2,1)} %get-tuple-element.9.rest_ref), custom_call_target="tpu_custom_call" | custom-call | flops 1000000 | bytes 2500000 | tf_op jit(solution)/shard_map/pallas_call | solution.py:549

commit v5 on v4

--- a/solution.py
+++ b/solution.py
@@ -220,7 +220,7 @@
             wait_copy(inb.at[qg, i], in_r.at[qg, i])
 
     def first(t, carried):
-        pair = [(r + 2 * t + step) % ROWS for step in range(2)]
+        pair = [(r + 4 * t + step) % ROWS for step in range(4)]
         for i in pair:
             arrive(K, Q, i)
         for i in pair:
@@ -241,7 +241,7 @@
                 local[0, i, chunk, :, cols] = top
                 local[1, i, chunk, :, cols] = jnp.sum(p, axis=0)
 
-    lax.fori_loop(0, ROWS // 2, first, 0)
+    lax.fori_loop(0, ROWS // 4, first, 0)
 
     def st_copy(part, d):
         return remote(
@@ -252,7 +252,7 @@
         cols = slice(part * HALF, (part + 1) * HALF)
 
         def second(t, carried):
-            pair = [(r + 2 * t + step) % ROWS for step in range(2)]
+            pair = [(r + 4 * t + step) % ROWS for step in range(4)]
             if part == 0:
                 for i in pair:
                     arrive(V, G, i)
@@ -273,7 +273,7 @@
                 wg_buf[i, rows, cols] = wg
                 local[2, i, chunk, :, cols] = jnp.sum(folded(p_buf[i, rows, cols] * wg), axis=0)
 
-        lax.fori_loop(0, ROWS // 2, second, 0)
+        lax.fori_loop(0, ROWS // 4, second, 0)
         tops = local[0, :, :, :, cols].reshape(ROWS, CHUNKS * LINES, HALF)
         top = jnp.max(tops, axis=1, keepdims=True)
         scale = jnp.exp2(tops - top)
@@ -364,15 +364,17 @@
                         dq_copy(t, y))
 
         def step(t, carried):
-            weights(2 * t, 0)
-            products(2 * t, 0)
-            weights(2 * t + 1, 1)
-            products(2 * t + 1, 1)
-            send_back(2 * t)
-            send_back(2 * t + 1)
+            for pair in range(2):
+                u = 4 * t + 2 * pair
+                weights(u, 0)
+                products(u, 0)
+                weights(u + 1, 1)
+                products(u + 1, 1)
+                send_back(u)
+                send_back(u + 1)
             return carried
 
-        lax.fori_loop(0, ROWS // 2, step, 0)
+        lax.fori_loop(0, ROWS // 4, step, 0)
         away = pl.ds(pl.multiple_of((1 - yl) * HALF, HALF), HALF)
         turned = flip(db_acc[rows, away]).astype(BF16)
         for cc in range(2):

time: 65 us -> 64.4 us (level); the launches traced: 64.1 us -> 64.3 us
  no operation moved by 1% of the time
where the time goes in v5:
time: 64.4 us; the launch traced here: 64.3 us
  Pallas kernels  63.6 us (99%)
    pallas_call x1, Pallas kernels, on_device(): pl.pallas_call(kernel, out_shape=(shape((3, 2, 2, HEAD_DIM, BLOCK), F32),...  61.3 us
    pallas_call x1, Pallas kernels, on_device(): pl.pallas_call(finish, out_shape=(pair, pair, pair, shape((HEADS, BLOCK,...  2.36 us

profile of v5, /device:TPU:1, one launch (start us, length us, event | category | flops | bytes accessed | tf_op | source)
XLA Modules:
  0.0 64.3 jit_solution(15138563936306941115)
XLA Ops:
  0.6 61.3 %shard_map.93 = (f32[3,2,2,32,128]{4,3,2,1,0:T(8,128)}, f32[128,512]{1,0:T(8,128)}, bf16[4,2,128,256]{3,2,1,0:T(8,128)(2,1)}) custom-call(bf16[1,128,128]{2,1,0:T(8,128)(2,1)} %q_ref.1, bf16[1,128,128]{2,1,0:T(8,128)(2,1)} %k_ref.1, bf16[1,128,128]{2,1,0:T(8,128)(2,1)} %v_ref.1, bf16[4,128,512]{2,1,0:T(8,128)(2,1)} %b_ref.1, s32[1,512]{1,0:T(1,128)} %bitcast.1, ...), custom_call_target="tpu_custom_call" | custom-call | flops 4000000000 | bytes 3000000 | tf_op jit(solution)/shard_map/pallas_call | solution.py:536
  61.9 2.4 %shard_map.94 = (f32[1,128,128]{2,1,0:T(8,128)}, f32[1,128,128]{2,1,0:T(8,128)}, f32[1,128,128]{2,1,0:T(8,128)}, f32[4,128,512]{2,1,0:T(8,128)}) custom-call(f32[3,2,2,32,128]{4,3,2,1,0:T(8,128)} %get-tuple-element.7.grads_ref, f32[128,512]{1,0:T(8,128)} %get-tuple-element.8.own_ref, bf16[4,2,128,256]{3,2,1,0:T(8,128)(2,1)} %get-tuple-element.9.rest_ref), custom_call_target="tpu_custom_call" | custom-call | flops 1000000 | bytes 2500000 | tf_op jit(solution)/shard_map/pallas_call | solution.py:551
